TPU v7x, 512 devices: a whole 4x4x16 slice. The times are simulated.
512 devices in a mesh: inner: 32 (over y, x, core), outer: 16 (over z).
Axes of the slice: x: 4, y: 4, z: 16, core: 2. Of those that a mesh axis runs over, the one named last changes fastest.
Arguments:
- activations: bfloat16 [131072, 8192], P(('inner', 'outer')), may hold values from -24 to 24
- output_grads: bfloat16 [131072, 512], P(('inner', 'outer')), may hold values from -0.015625 to 0.015625
Outputs:
- weight_grad: float32 [8192, 512], P(('inner', 'outer'))
All inputs are finite; a program needn't handle non-finite values.
Results may differ from a plain program's by a relative error of at most 0.0055.
The roundings to bfloat16 on the way count: a program that leaves them out, or rounds other values in their place, can miss the bound.
Values may be sent and summed in bfloat16 or wider, within the bound.
No kernel may reach another device: no remote copies, remote signals or barrier semaphores. Data moves between devices by JAX's collectives and lax.ppermute only.
A program may use at most 192 MiB of HBM per device.

v0:
```python
import jax
import jax.numpy as jnp
from jax import lax
from jax.sharding import PartitionSpec as P

BLOCK = 128


def to_grid(values):
    magnitude = jnp.abs(values)
    spacing = jnp.full_like(values, 2.0 ** (-9))
    for power in range(-5, 9):
        spacing = jnp.where(magnitude >= 2.0**power, 2.0 ** (power - 3), spacing)
    return jnp.floor(values / spacing + 0.5) * spacing


def quantize(blocks):
    scale = ((jnp.max(jnp.abs(blocks), axis=-1) + 1e-06) / 448.0).astype(jnp.bfloat16)
    widened = lax.optimization_barrier(scale).astype(jnp.float32)
    codes = to_grid(blocks / widened[..., None]).astype(jnp.bfloat16)
    return (codes, scale)


def source_sum(codes, scale):
    return jnp.sum(codes.astype(jnp.float32) * scale.astype(jnp.float32)[..., None], axis=0)


def shards(activations, output_grads):
    n_inner = lax.axis_size("inner")
    n_outer = lax.axis_size("outer")
    width = activations.shape[1]
    cols = output_grads.shape[1]
    n_blocks = cols // BLOCK
    own_rows = width // n_inner
    last_rows = own_rows // n_outer
    local = lax.dot_general(
        activations, output_grads, (((0,), (0,)), ((), ())), preferred_element_type=jnp.float32
    )
    codes, scale = quantize(local.reshape(n_inner, own_rows, n_blocks, BLOCK))
    got_codes, got_scale = (
        lax.all_to_all(codes, "inner", split_axis=0, concat_axis=0, tiled=True),
        lax.all_to_all(scale, "inner", split_axis=0, concat_axis=0, tiled=True),
    )
    group_sum = source_sum(got_codes, got_scale)
    codes2, scale2 = quantize(group_sum.reshape(n_outer, last_rows, n_blocks, BLOCK))
    fin_codes, fin_scale = (
        lax.all_to_all(codes2, "outer", split_axis=0, concat_axis=0, tiled=True),
        lax.all_to_all(scale2, "outer", split_axis=0, concat_axis=0, tiled=True),
    )
    return source_sum(fin_codes, fin_scale).reshape(last_rows, cols)


def solution(mesh):
    return jax.shard_map(
        shards,
        mesh=mesh,
        in_specs=(P(("inner", "outer"), None), P(("inner", "outer"), None)),
        out_specs=P(("inner", "outer"), None),
        check_vma=False,
    )
```

profile of v0, /device:TPU:32, one launch (start us, length us, event | category | flops | bytes accessed | tf_op | source)
XLA Modules:
  0.0 278.0 jit_solution(1182111334655294509)
XLA Ops:
  0.0 0.0 copy-start
  0.0 0.9 copy-done
  1.0 10.3 %fusion = f32[8192,512]{1,0:T(8,128)} fusion(bf16[256,8192]{1,0:T(8,128)(2,1)} %param.2, bf16[256,512]{1,0:T(8,128)(2,1)S(1)} %copy-done), kind=kOutput, calls=%fused_computation.13 | convolution fusion | flops 2147483648 | bytes 21233664 | tf_op jit(solution)/shard_map/dot_general | solution.py:36
  11.2 19.2 %reshape.19 = f32[32,256,4,128]{3,2,1,0:T(4,128)} reshape(f32[8192,512]{1,0:T(8,128)} %fusion) | data formatting | bytes 33554432 | tf_op jit(solution)/shard_map/reshape | solution.py:39
  30.5 14.6 %abs_reduce_fusion = f32[32,256,4]{2,1,0:T(8,128)} fusion(f32[32,256,4,128]{3,2,1,0:T(4,128)} %reshape.19), kind=kLoop, calls=%fused_computation.4 | loop fusion | flops 8355840 | bytes 16908288 | tf_op jit(solution)/shard_map/reduce_max | solution.py:18
  45.1 2.9 %copy.34 = f32[32,256,4]{1,0,2:T(8,128)S(1)} copy(f32[32,256,4]{2,1,0:T(8,128)} %abs_reduce_fusion) | data formatting | bytes 262144 | tf_op jit(solution)/shard_map/reduce_max | solution.py:18
  48.0 0.7 copy.36
  48.6 7.3 %all-to-all-start.1 = ((bf16[32,256,4]{1,2,0:T(4,128)(2,1)}), bf16[32,256,4]{1,2,0:T(4,128)(2,1)S(1)}, u32[]{:S(2)}, u32[]{:S(2)}) async-start(bf16[32,256,4]{1,2,0:T(4,128)(2,1)} %copy.36), calls=%async_computation.1 | async-start | bytes 131072 | tf_op jit(solution)/shard_map/all_to_all | solution.py:42
  56.0 2.4 copy.35
  58.4 0.0 copy-start.1
  58.4 46.6 %multiply_convert_fusion = bf16[32,256,4,128]{3,2,1,0:T(4,128)(2,1)} fusion(f32[32,256,4,128]{3,2,1,0:T(4,128)} %reshape.19, f32[32,256,4]{2,1,0:T(8,128)} %copy.35), kind=kLoop, calls=%fused_computation.1 | loop fusion | flops 150994944 | bytes 25296896 | tf_op jit(solution)/shard_map/convert_element_type | solution.py:20
  105.0 0.0 all-to-all-done.1
  105.0 7.5 %all-to-all-start = ((bf16[32,256,4,128]{3,2,1,0:T(4,128)(2,1)}), bf16[32,256,4,128]{3,2,1,0:T(4,128)(2,1)}, u32[]{:S(2)}, u32[]{:S(2)}) async-start(bf16[32,256,4,128]{3,2,1,0:T(4,128)(2,1)} %multiply_convert_fusion), calls=%async_computation | async-start | bytes 16777216 | tf_op jit(solution)/shard_map/all_to_all | solution.py:41
  112.5 2.7 copy.38
  115.2 103.2 %all-to-all-done = bf16[32,256,4,128]{3,2,1,0:T(4,128)(2,1)} async-done(((bf16[32,256,4,128]{3,2,1,0:T(4,128)(2,1)}), bf16[32,256,4,128]{3,2,1,0:T(4,128)(2,1)}, u32[]{:S(2)}, u32[]{:S(2)}) %all-to-all-start) | async-done | bytes 8388640 | tf_op jit(solution)/shard_map/all_to_all | solution.py:41
  218.4 11.6 %multiply_reduce_fusion = f32[256,4,128]{2,1,0:T(4,128)S(1)} fusion(bf16[32,256,4,128]{3,2,1,0:T(4,128)(2,1)} %all-to-all-done, f32[32,256,4]{2,1,0:T(8,128)} %copy.38), kind=kLoop, calls=%fused_computation | loop fusion | flops 12451840 | bytes 9043968 | tf_op jit(solution)/shard_map/reduce_sum | solution.py:25
  230.0 0.2 abs_reduce_fusion.1
  230.2 0.1 convert_element_type.39
  230.3 0.6 copy.42
  230.9 15.2 %all-to-all-start.3 = ((bf16[16,16,4]{1,2,0:T(4,128)(2,1)}), bf16[16,16,4]{1,2,0:T(4,128)(2,1)S(1)}, u32[]{:S(2)}, u32[]{:S(2)}) async-start(bf16[16,16,4]{1,2,0:T(4,128)(2,1)} %copy.42), calls=%async_computation.3 | async-start | bytes 32768 | tf_op jit(solution)/shard_map/all_to_all | solution.py:48
  246.1 0.7 multiply_convert_fusion.1
  246.9 0.7 copy.41
  247.6 9.8 %all-to-all-done.3 = bf16[16,16,4]{1,2,0:T(4,128)(2,1)S(1)} async-done(((bf16[16,16,4]{1,2,0:T(4,128)(2,1)}), bf16[16,16,4]{1,2,0:T(4,128)(2,1)S(1)}, u32[]{:S(2)}, u32[]{:S(2)}) %all-to-all-start.3) | async-done | bytes 2080 | tf_op jit(solution)/shard_map/all_to_all | solution.py:48
  257.4 4.7 %all-to-all-start.2 = ((bf16[16,16,4,128]{3,1,2,0:T(8,128)(2,1)}), bf16[16,16,4,128]{3,1,2,0:T(8,128)(2,1)S(1)}, u32[]{:S(2)}, u32[]{:S(2)}) async-start(bf16[16,16,4,128]{3,1,2,0:T(8,128)(2,1)} %copy.41), calls=%async_computation.2 | async-start | bytes 524288 | tf_op jit(solution)/shard_map/all_to_all | solution.py:47
  262.1 15.1 %all-to-all-done.2 = bf16[16,16,4,128]{3,1,2,0:T(8,128)(2,1)S(1)} async-done(((bf16[16,16,4,128]{3,1,2,0:T(8,128)(2,1)}), bf16[16,16,4,128]{3,1,2,0:T(8,128)(2,1)S(1)}, u32[]{:S(2)}, u32[]{:S(2)}) %all-to-all-start.2) | async-done | bytes 262176 | tf_op jit(solution)/shard_map/all_to_all | solution.py:47
  277.2 0.2 multiply_reduce_fusion.1
  277.4 0.6 copy_bitcast_fusion
  278.0 0.0 copy-done.1
  (5 shorter events, 0.0 us)
Async XLA Ops:
  0.0 1.0 copy-start
  48.6 56.3 %all-to-all-start.1 = ((bf16[32,256,4]{1,2,0:T(4,128)(2,1)}), bf16[32,256,4]{1,2,0:T(4,128)(2,1)S(1)}, u32[]{:S(2)}, u32[]{:S(2)}) async-start(bf16[32,256,4]{1,2,0:T(4,128)(2,1)} %copy.36), calls=%async_computation.1 | async-start | bytes 131072 | tf_op jit(solution)/shard_map/all_to_all | solution.py:42
  58.4 219.6 %copy-start.1 = (bf16[256,512]{1,0:T(8,128)(2,1)S(1)}, bf16[256,512]{1,0:T(8,128)(2,1)}, u32[]{:S(2)}) copy-start(bf16[256,512]{1,0:T(8,128)(2,1)} %param.3) | copy-start | bytes 786436
  105.0 113.4 %all-to-all-start = ((bf16[32,256,4,128]{3,2,1,0:T(4,128)(2,1)}), bf16[32,256,4,128]{3,2,1,0:T(4,128)(2,1)}, u32[]{:S(2)}, u32[]{:S(2)}) async-start(bf16[32,256,4,128]{3,2,1,0:T(4,128)(2,1)} %multiply_convert_fusion), calls=%async_computation | async-start | bytes 16777216 | tf_op jit(solution)/shard_map/all_to_all | solution.py:41
  230.9 26.5 %all-to-all-start.3 = ((bf16[16,16,4]{1,2,0:T(4,128)(2,1)}), bf16[16,16,4]{1,2,0:T(4,128)(2,1)S(1)}, u32[]{:S(2)}, u32[]{:S(2)}) async-start(bf16[16,16,4]{1,2,0:T(4,128)(2,1)} %copy.42), calls=%async_computation.3 | async-start | bytes 32768 | tf_op jit(solution)/shard_map/all_to_all | solution.py:48
  257.4 19.8 %all-to-all-start.2 = ((bf16[16,16,4,128]{3,1,2,0:T(8,128)(2,1)}), bf16[16,16,4,128]{3,1,2,0:T(8,128)(2,1)S(1)}, u32[]{:S(2)}, u32[]{:S(2)}) async-start(bf16[16,16,4,128]{3,1,2,0:T(8,128)(2,1)} %copy.41), calls=%async_computation.2 | async-start | bytes 524288 | tf_op jit(solution)/shard_map/all_to_all | solution.py:47
where the time goes:
time: 279 us; the launch traced here: 278 us
  waiting for transfers between devices  128 us (46%)
  other arithmetic  74 us (27%)
  starting transfers between devices  34.7 us (12%)
  local copies, waits for them, and re-layouts  30.8 us (11%)
  matrix products  10.3 us (4%)
    all_to_all x1, waiting for transfers between devices, shards(): lax.all_to_all(codes, 'inner', split_axis=0, concat_axis=0, tiled=True)  103 us
    convert_element_type x2, other arithmetic, quantize(): codes = to_grid(blocks / widened[..., None]).astype(jnp.bfloat16)  47.3 us
    reshape x1, local copies, waits for them, and re-layouts, shards(): codes, scale = quantize(local.reshape(n_inner, own_rows, n_blocks, BLOCK))  19.2 us
    all_to_all x1, starting transfers between devices, shards(): lax.all_to_all(scale2, 'outer', split_axis=0, concat_axis=0, tiled=True)  15.2 us
    all_to_all x1, waiting for transfers between devices, shards(): lax.all_to_all(codes2, 'outer', split_axis=0, concat_axis=0, tiled=True)  15.1 us
    reduce_max x2, other arithmetic, quantize(): jnp.max(jnp.abs(blocks), axis=-1) + 1e-06  14.8 us
    reduce_sum x2, other arithmetic, source_sum(): jnp.sum(codes.astype(jnp.float32) * scale.astype(jnp.float32)[..., None],...  11.8 us
    dot_general x1, matrix products, shards(): lax.dot_general(activations, output_grads, (((0,), (0,)), ((), ())), pref...  10.3 us
  transfers between devices with their start and end apart: 4, of which 3 were waited for; matrix products, arithmetic and copies ran while one was open for 19% of the time, Pallas kernels for 0%

commit v1 on v0

v1 whole, which is shorter than its diff:
```python
import functools
import math

import jax
import jax.numpy as jnp
from jax import lax
from jax.experimental import pallas as pl
from jax.experimental.pallas import tpu as pltpu
from jax.sharding import PartitionSpec as P

BLOCK = 128
COLS = 512
NBLK = COLS // BLOCK
PART = 256
NX = 4
NY = 4
TAIL = 16
F32 = jnp.float32
BF16 = jnp.bfloat16
SPAN = 124.0 * math.log(2.0)


def to_grid(x):
    x = x + jnp.abs(x) * (2.0**-22)
    c = x * (2.0**20 + 1.0)
    fine = c - (c - x)
    coarse = (x + 24576.0) - 24576.0
    return jnp.where(jnp.abs(x) < 2.0**-6, coarse, fine)


def quantize(g):
    top = jnp.max(jnp.abs(g), axis=0, keepdims=True)
    scale = ((top + 1e-06) / 448.0).astype(BF16).astype(F32)
    return to_grid(g * (1.0 / scale)), scale


def encode(s):
    mag = jnp.abs(s)
    top = jnp.max(mag, axis=0, keepdims=True)
    norm = (top * 1.004 + 1e-30).astype(BF16)
    y = jnp.exp(mag * ((2.0 * SPAN) / norm.astype(F32)) - SPAN)
    return jnp.where(s < 0, -y, y).astype(BF16), norm


def decode(code, norm):
    y = code.astype(F32)
    mag = (jnp.log(jnp.abs(y)) + SPAN) * (norm.astype(F32) * (0.5 / SPAN))
    return jnp.where(y < 0, -mag, mag)


def rows_of(b):
    return pl.ds(b * BLOCK, BLOCK)


def pair_block(gto, gtp, ao, ap, b):
    total = None
    for gt, a in ((gto, ao), (gtp, ap)):
        local = jnp.dot(gt[rows_of(b), :], a[...], preferred_element_type=F32)
        codes, scale = quantize(local)
        part = codes * scale
        total = part if total is None else total + part
    return total


def put_coded(out, totals):
    norms = []
    for b, total in enumerate(totals):
        code, norm = encode(total)
        out[rows_of(b), :] = code
        norms.append(norm.astype(F32))
    n = norms[0].shape[1]
    out[COLS : COLS + TAIL, :] = jnp.concatenate(
        norms + [jnp.zeros((TAIL - NBLK, n), F32)], axis=0
    ).astype(BF16)


def get_coded(ref, b):
    return decode(ref[rows_of(b), :], ref[COLS + b : COLS + b + 1, :])


def pair_sent_kernel(tab, gto, gtp, ao, ap, out):
    put_coded(out, [pair_block(gto, gtp, ao, ap, b) for b in range(NBLK)])


def pair_kept_kernel(tab, gto, gtp, ao, ap, out):
    for b in range(NBLK):
        out[rows_of(b), :] = pair_block(gto, gtp, ao, ap, b)


def pair_sum(kept, tab, gto, gtp, a_own, a_par):
    tok = a_own.shape[0]
    whole = pl.BlockSpec((COLS, tok), lambda q, tab: (0, 0))
    part = pl.BlockSpec((tok, PART), lambda q, tab: (0, tab[q]))
    height = COLS if kept else COLS + TAIL
    return pl.pallas_call(
        pair_kept_kernel if kept else pair_sent_kernel,
        grid_spec=pltpu.PrefetchScalarGridSpec(
            num_scalar_prefetch=1,
            grid=(4,),
            in_specs=[whole, whole, part, part],
            out_specs=pl.BlockSpec((height, PART), lambda q, tab: (0, q)),
        ),
        out_shape=jax.ShapeDtypeStruct((height, 4 * PART), F32 if kept else BF16),
        compiler_params=pltpu.CompilerParams(vmem_limit_bytes=48 * 2**20),
        cost_estimate=pl.CostEstimate(
            flops=4 * COLS * tok * 4 * PART, bytes_accessed=3 * 2**20, transcendentals=2**19
        ),
    )(tab, gto, gtp, a_own, a_par)


def level2_kernel(tab, own, r1, r2, r3, out):
    totals = []
    for b in range(NBLK):
        total = own[rows_of(b), :]
        for r in (r1, r2, r3):
            total = total + get_coded(r, b)
        totals.append(total)
    put_coded(out, totals)


def part_specs():
    return [pl.BlockSpec((COLS, PART), lambda i, tab: (0, tab[0]))] + [
        pl.BlockSpec((COLS + TAIL, PART), lambda i, tab: (0, tab[0]))
    ] * 3


def level2_sent(tab, own, got):
    return pl.pallas_call(
        level2_kernel,
        grid_spec=pltpu.PrefetchScalarGridSpec(
            num_scalar_prefetch=1,
            grid=(1,),
            in_specs=part_specs(),
            out_specs=pl.BlockSpec((COLS + TAIL, PART), lambda i, tab: (0, 0)),
        ),
        out_shape=jax.ShapeDtypeStruct((COLS + TAIL, PART), BF16),
        compiler_params=pltpu.CompilerParams(vmem_limit_bytes=48 * 2**20),
    )(tab, own, *got)


def group_kernel(tab, own, r1, r2, r3, s1, s2, s3, out):
    n = own.shape[1]
    n_outer = out.shape[0]
    rows = n // n_outer
    scales = []
    for b in range(NBLK):
        total = own[rows_of(b), :]
        for r in (r1, r2, r3, s1, s2, s3):
            total = total + get_coded(r, b)
        codes, scale = quantize(total)
        scales.append(scale)
        out[:, b * rows : (b + 1) * rows, :] = codes.T.astype(BF16).reshape(n_outer, rows, BLOCK)
    wide = jnp.concatenate(scales + [jnp.zeros((BLOCK - NBLK, n), F32)], axis=0)
    out[:, NBLK * rows :, :] = wide.T.astype(BF16).reshape(n_outer, rows, BLOCK)


def group_codes(tab, own, got, got2, n_outer):
    shape = (n_outer, (NBLK + 1) * (PART // n_outer), BLOCK)
    return pl.pallas_call(
        group_kernel,
        grid_spec=pltpu.PrefetchScalarGridSpec(
            num_scalar_prefetch=1,
            grid=(1,),
            in_specs=part_specs()
            + [pl.BlockSpec((COLS + TAIL, PART), lambda i, tab: (0, 0))] * 3,
            out_specs=pl.BlockSpec(shape, lambda i, tab: (0, 0, 0)),
        ),
        out_shape=jax.ShapeDtypeStruct(shape, BF16),
        compiler_params=pltpu.CompilerParams(vmem_limit_bytes=48 * 2**20),
    )(tab, own, *got, *got2)


def final_kernel(got, out):
    rows = out.shape[0]
    for b in range(NBLK):
        total = jnp.zeros((rows, BLOCK), F32)
        for s in range(got.shape[0]):
            scale = got[s, NBLK * rows :, b : b + 1].astype(F32)
            total = total + got[s, b * rows : (b + 1) * rows, :].astype(F32) * scale
        out[:, b * BLOCK : (b + 1) * BLOCK] = total


def final_sum(got):
    rows = got.shape[1] // (NBLK + 1)
    return pl.pallas_call(
        final_kernel,
        out_shape=jax.ShapeDtypeStruct((rows, COLS), F32),
        compiler_params=pltpu.CompilerParams(vmem_limit_bytes=48 * 2**20),
    )(got)


def index_of(y, x, c):
    return ((y % NY) * NX + x % NX) * 2 + c


def ring(first, k):
    pairs = []
    for y in range(NY):
        for x in range(NX):
            for c in range(2):
                along_x = (c == 0) == first
                to = index_of(y, x + k, c) if along_x else index_of(y + k, x, c)
                pairs.append((index_of(y, x, c), to))
    return pairs


def shards(activations, output_grads):
    me = lax.axis_index("inner")
    n_outer = lax.axis_size("outer")
    c, x, y = me % 2, (me // 2) % NX, me // (2 * NX)
    swap = [(i, i ^ 1) for i in range(2 * NX * NY)]
    g_par = lax.ppermute(output_grads, "inner", swap)
    a_par = lax.ppermute(activations, "inner", swap)
    gto, gtp = output_grads.T, g_par.T

    def column_parts(k):
        q = jnp.arange(4, dtype=jnp.int32)
        return 2 * jnp.where(c == 0, q * NX + (x + k) % NX, ((y + k) % NY) * NX + q) + c

    got = []
    for k in (2, 1, 3):
        coded = pair_sum(False, column_parts(k), gto, gtp, activations, a_par)
        got.append(lax.ppermute(coded, "inner", ring(True, k)))
    own = pair_sum(True, column_parts(0), gto, gtp, activations, a_par)
    base = jnp.where(c == 0, y, x)

    def part_of(k):
        return ((base + k) % 4).astype(jnp.int32).reshape(1)

    got2 = []
    for k in (2, 1, 3):
        coded = level2_sent(part_of(k), own, got)
        got2.append(lax.ppermute(coded, "inner", ring(False, k)))
    packed = group_codes(part_of(0), own, got, got2, n_outer)
    return final_sum(lax.all_to_all(packed, "outer", split_axis=0, concat_axis=0, tiled=True))


def solution(mesh):
    return jax.shard_map(
        shards,
        mesh=mesh,
        in_specs=(P(("inner", "outer"), None), P(("inner", "outer"), None)),
        out_specs=P(("inner", "outer"), None),
        check_vma=False,
    )
```

time: 279 us -> 120 us (0.43)
  the two profiles are of different devices: /device:TPU:32 before, /device:TPU:62 now
where the time goes in v1:
time: 120 us; the launch traced here: 119 us
  Pallas kernels  36 us (30%)
  blocking collectives  33.5 us (28%)
  starting transfers between devices  22.5 us (19%)
  waiting for transfers between devices  22.4 us (19%)
  local copies, waits for them, and re-layouts  4.32 us (4%)
    all_to_all x1, blocking collectives, shards(): lax.all_to_all(packed, 'outer', split_axis=0, concat_axis=0, tiled=True)  33.5 us
    pallas_call x4, Pallas kernels, pair_sum(): pl.pallas_call(pair_kept_kernel if kept else pair_sent_kernel, grid_spec=...  24.2 us
    ppermute x3, waiting for transfers between devices, shards(): got.append(lax.ppermute(coded, 'inner', ring(True, k)))  10.5 us
    ppermute x3, starting transfers between devices, shards(): got.append(lax.ppermute(coded, 'inner', ring(True, k)))  9.21 us
    ppermute x3, starting transfers between devices, shards(): got2.append(lax.ppermute(coded, 'inner', ring(False, k)))  8.95 us
    pallas_call x3, Pallas kernels, level2_sent(): pl.pallas_call(level2_kernel, grid_spec=pltpu.PrefetchScalarGridSpec(num_...  8.37 us
    ppermute x3, waiting for transfers between devices, shards(): got2.append(lax.ppermute(coded, 'inner', ring(False, k)))  8.1 us
    unnamed x9, local copies, waits for them, and re-layouts  4.32 us
  transfers between devices with their start and end apart: 8, of which 4 were waited for; matrix products, arithmetic and copies ran while one was open for 1% of the time, Pallas kernels for 20%

profile of v1, /device:TPU:62, one launch (start us, length us, event | category | flops | bytes accessed | tf_op | source)
XLA Modules:
  0.0 119.1 jit_solution(4822150927277041008)
XLA Ops:
  0.0 1.9 %collective-permute-start.1 = (bf16[256,8192]{1,0:T(8,128)(2,1)}, bf16[256,8192]{1,0:T(8,128)(2,1)}, u32[]{:S(2)}, u32[]{:S(2)}) collective-permute-start(bf16[256,8192]{1,0:T(8,128)(2,1)} %ao.7), channel_id=1, source_target_pairs={{0,16},{16,0},{32,48},{48,32},{64,80},{80,64},{96,112},{112,96},{1... | collective-permute-start | bytes 12582920 | tf_op jit(solution)/shard_map/ppermute | solution.py:213
  1.9 1.1 copy.3
  3.0 2.4 %collective-permute-start = (bf16[256,512]{0,1:T(8,128)(2,1)S(1)}, bf16[256,512]{0,1:T(8,128)(2,1)S(1)}, u32[]{:S(2)}, u32[]{:S(2)}) collective-permute-start(bf16[256,512]{0,1:T(8,128)(2,1)S(1)} %copy.3), channel_id=1, source_target_pairs={{0,16},{16,0},{32,48},{48,32},{64,80},{80,64},{96,112},{112,96},{1... | collective-permute-start | bytes 786440 | tf_op jit(solution)/shard_map/ppermute | solution.py:212
  5.6 3.8 %collective-permute-done = bf16[256,512]{0,1:T(8,128)(2,1)S(1)} collective-permute-done((bf16[256,512]{0,1:T(8,128)(2,1)S(1)}, bf16[256,512]{0,1:T(8,128)(2,1)S(1)}, u32[]{:S(2)}, u32[]{:S(2)}) %collective-permute-start) | collective-permute-done | bytes 262176 | tf_op jit(solution)/shard_map/ppermute | solution.py:212
  9.4 0.0 collective-permute-done.1.ap
  9.4 2.3 %copy-done = bf16[256,8192]{1,0:T(8,128)(2,1)S(1)} copy-done((bf16[256,8192]{1,0:T(8,128)(2,1)S(1)}, bf16[256,8192]{1,0:T(8,128)(2,1)}, u32[]{:S(2)}) %copy-start) | copy-done | bytes 4194328
  11.7 6.4 %shard_map.29 = bf16[528,1024]{1,0:T(8,128)(2,1)} custom-call(s32[4]{0:T(128)S(1)} %fusion.3.tab, bf16[512,256]{1,0:T(8,128)(2,1)S(1)} %bitcast.6, bf16[512,256]{1,0:T(8,128)(2,1)S(1)} %bitcast.10, bf16[256,8192]{1,0:T(8,128)(2,1)S(1)} %copy-done, bf16[256,8192]{1,0:T(8,128)(2,1)} %collective-permute-done.1.ap), custom_call_target="tpu_custom_call" | custom-call | flops 536870912 | bytes 3145728 | tf_op jit(solution)/shard_map/pallas_call | solution.py:95
  18.1 3.3 %collective-permute-start.2 = (bf16[528,1024]{1,0:T(8,128)(2,1)}, bf16[528,1024]{1,0:T(8,128)(2,1)S(1)}, u32[]{:S(2)}, u32[]{:S(2)}) collective-permute-start(bf16[528,1024]{1,0:T(8,128)(2,1)} %shard_map.29), channel_id=1, source_target_pairs={{0,64},{16,272},{32,96},{48,304},{64,0},{80,336},{96,32},{112,368}... | collective-permute-start | bytes 3244040 | tf_op jit(solution)/shard_map/ppermute | solution.py:223
  21.4 6.4 %shard_map.30 = bf16[528,1024]{1,0:T(8,128)(2,1)} custom-call(s32[4]{0:T(128)S(1)} %fusion.5.tab, bf16[512,256]{1,0:T(8,128)(2,1)S(1)} %bitcast.7, bf16[512,256]{1,0:T(8,128)(2,1)S(1)} %bitcast.11, bf16[256,8192]{1,0:T(8,128)(2,1)S(1)} %copy-done, bf16[256,8192]{1,0:T(8,128)(2,1)} %collective-permute-done.1.ap), custom_call_target="tpu_custom_call" | custom-call | flops 536870912 | bytes 3145728 | tf_op jit(solution)/shard_map/pallas_call | solution.py:95
  27.8 4.0 %collective-permute-start.3 = (bf16[528,1024]{1,0:T(8,128)(2,1)}, bf16[528,1024]{1,0:T(8,128)(2,1)}, u32[]{:S(2)}, u32[]{:S(2)}) collective-permute-start(bf16[528,1024]{1,0:T(8,128)(2,1)} %shard_map.30), channel_id=1, source_target_pairs={{0,32},{16,144},{32,64},{48,176},{64,96},{80,208},{96,0},{112,240}... | collective-permute-start | bytes 3244040 | tf_op jit(solution)/shard_map/ppermute | solution.py:223
  31.8 0.0 copy-done.2
  31.8 6.4 %shard_map.31 = bf16[528,1024]{1,0:T(8,128)(2,1)} custom-call(s32[4]{0:T(128)S(1)} %fusion.7.tab, bf16[512,256]{1,0:T(8,128)(2,1)S(1)} %bitcast.8, bf16[512,256]{1,0:T(8,128)(2,1)S(1)} %bitcast.12, bf16[256,8192]{1,0:T(8,128)(2,1)S(1)} %copy-done, bf16[256,8192]{1,0:T(8,128)(2,1)} %collective-permute-done.1.ap), custom_call_target="tpu_custom_call" | custom-call | flops 536870912 | bytes 3145728 | tf_op jit(solution)/shard_map/pallas_call | solution.py:95
  38.1 1.9 %collective-permute-start.4 = (bf16[528,1024]{1,0:T(8,128)(2,1)}, bf16[528,1024]{1,0:T(8,128)(2,1)}, u32[]{:S(2)}, u32[]{:S(2)}) collective-permute-start(bf16[528,1024]{1,0:T(8,128)(2,1)} %shard_map.31), channel_id=1, source_target_pairs={{0,96},{16,400},{32,0},{48,432},{64,32},{80,464},{96,64},{112,496}... | collective-permute-start | bytes 3244040 | tf_op jit(solution)/shard_map/ppermute | solution.py:223
  40.2 0.0 copy-start.3
  40.2 0.9 copy-done.3
  41.1 5.0 %shard_map.28.own = f32[512,1024]{1,0:T(8,128)S(1)} custom-call(s32[4]{0:T(128)S(1)} %fusion.1.tab, bf16[512,256]{1,0:T(8,128)(2,1)S(1)} %bitcast.9, bf16[512,256]{1,0:T(8,128)(2,1)S(1)} %bitcast.13, bf16[256,8192]{1,0:T(8,128)(2,1)} %ao.7, bf16[256,8192]{1,0:T(8,128)(2,1)} %collective-permute-done.1.ap), custom_call_target="tpu_custom_call" | custom-call | flops 536870912 | bytes 3145728 | tf_op jit(solution)/shard_map/pallas_call | solution.py:95
  46.2 0.0 copy-start.1
  46.2 0.0 collective-permute-done.2.r1
  46.2 0.2 collective-permute-done.3.r2
  46.3 10.4 %collective-permute-done.4.r3 = bf16[528,1024]{1,0:T(8,128)(2,1)} collective-permute-done((bf16[528,1024]{1,0:T(8,128)(2,1)}, bf16[528,1024]{1,0:T(8,128)(2,1)}, u32[]{:S(2)}, u32[]{:S(2)}) %collective-permute-start.4) | collective-permute-done | bytes 1081376 | tf_op jit(solution)/shard_map/ppermute | solution.py:223
  56.7 2.8 %shard_map.34 = bf16[528,256]{1,0:T(8,128)(2,1)} custom-call(s32[1]{0:T(128)} %bitcast.5.tab, f32[512,1024]{1,0:T(8,128)S(1)} %shard_map.28.own, bf16[528,1024]{1,0:T(8,128)(2,1)S(1)} %collective-permute-done.2.r1, bf16[528,1024]{1,0:T(8,128)(2,1)} %collective-permute-done.3.r2, bf16[528,1024]{1,0:T(8,128)(2,1)} %collective-permute-done.4.r3), custom_call_target="tpu_custom_call" | custom-call | tf_op jit(solution)/shard_map/pallas_call | solution.py:128
  59.5 2.6 %collective-permute-start.7 = (bf16[528,256]{1,0:T(8,128)(2,1)}, bf16[528,256]{1,0:T(8,128)(2,1)S(1)}, u32[]{:S(2)}, u32[]{:S(2)}) collective-permute-start(bf16[528,256]{1,0:T(8,128)(2,1)} %shard_map.34), channel_id=1, source_target_pairs={{0,384},{16,112},{32,416},{48,16},{64,448},{80,48},{96,480},{112,8... | collective-permute-start | bytes 811016 | tf_op jit(solution)/shard_map/ppermute | solution.py:233
  62.1 2.8 %shard_map.33 = bf16[528,256]{1,0:T(8,128)(2,1)} custom-call(s32[1]{0:T(128)} %bitcast.4.tab, f32[512,1024]{1,0:T(8,128)S(1)} %shard_map.28.own, bf16[528,1024]{1,0:T(8,128)(2,1)S(1)} %collective-permute-done.2.r1, bf16[528,1024]{1,0:T(8,128)(2,1)} %collective-permute-done.3.r2, bf16[528,1024]{1,0:T(8,128)(2,1)} %collective-permute-done.4.r3), custom_call_target="tpu_custom_call" | custom-call | tf_op jit(solution)/shard_map/pallas_call | solution.py:128
  64.9 4.4 %collective-permute-start.6 = (bf16[528,256]{1,0:T(8,128)(2,1)}, bf16[528,256]{1,0:T(8,128)(2,1)}, u32[]{:S(2)}, u32[]{:S(2)}) collective-permute-start(bf16[528,256]{1,0:T(8,128)(2,1)} %shard_map.33), channel_id=1, source_target_pairs={{0,128},{16,48},{32,160},{48,80},{64,192},{80,112},{96,224},{112,1... | collective-permute-start | bytes 811016 | tf_op jit(solution)/shard_map/ppermute | solution.py:233
  69.3 2.8 %shard_map.32 = bf16[528,256]{1,0:T(8,128)(2,1)} custom-call(s32[1]{0:T(128)} %bitcast.3.tab, f32[512,1024]{1,0:T(8,128)S(1)} %shard_map.28.own, bf16[528,1024]{1,0:T(8,128)(2,1)S(1)} %collective-permute-done.2.r1, bf16[528,1024]{1,0:T(8,128)(2,1)} %collective-permute-done.3.r2, bf16[528,1024]{1,0:T(8,128)(2,1)} %collective-permute-done.4.r3), custom_call_target="tpu_custom_call" | custom-call | tf_op jit(solution)/shard_map/pallas_call | solution.py:128
  72.1 1.9 %collective-permute-start.5 = (bf16[528,256]{1,0:T(8,128)(2,1)}, bf16[528,256]{1,0:T(8,128)(2,1)S(1)}, u32[]{:S(2)}, u32[]{:S(2)}) collective-permute-start(bf16[528,256]{1,0:T(8,128)(2,1)} %shard_map.32), channel_id=1, source_target_pairs={{0,256},{16,80},{32,288},{48,112},{64,320},{80,16},{96,352},{112,4... | collective-permute-start | bytes 811016 | tf_op jit(solution)/shard_map/ppermute | solution.py:233
  74.1 0.0 collective-permute-done.7.s3
  74.1 0.0 collective-permute-done.6.s2
  74.1 8.1 %collective-permute-done.5.s1 = bf16[528,256]{1,0:T(8,128)(2,1)S(1)} collective-permute-done((bf16[528,256]{1,0:T(8,128)(2,1)}, bf16[528,256]{1,0:T(8,128)(2,1)S(1)}, u32[]{:S(2)}, u32[]{:S(2)}) %collective-permute-start.5) | collective-permute-done | bytes 270368 | tf_op jit(solution)/shard_map/ppermute | solution.py:233
  82.2 2.7 %shard_map.35 = bf16[16,80,128]{2,1,0:T(8,128)(2,1)S(1)} custom-call(s32[1]{0:T(128)} %bitcast.tab, f32[512,1024]{1,0:T(8,128)} %copy-done.1, bf16[528,1024]{1,0:T(8,128)(2,1)S(1)} %collective-permute-done.2.r1, bf16[528,1024]{1,0:T(8,128)(2,1)} %collective-permute-done.3.r2, bf16[528,1024]{1,0:T(8,128)(2,1)} %collective-permute-done.4.r3, ...), custom_call_target="tpu_custom_call" | custom-call | tf_op jit(solution)/shard_map/pallas_call | solution.py:159
  84.9 33.5 %all_to_all.5.got = bf16[16,80,128]{2,1,0:T(8,128)(2,1)S(1)} all-to-all(bf16[16,80,128]{2,1,0:T(8,128)(2,1)S(1)} %shard_map.35), channel_id=1, replica_groups=mesh['inner'=32,'outer'=16] {'outer'}, dimensions={0} | all-to-all | bytes 655360 | tf_op jit(solution)/shard_map/all_to_all | solution.py:235
  118.3 0.8 shard_map.36
  (7 shorter events, 0.0 us)
Async XLA Ops:
  0.0 9.4 %collective-permute-start.1 = (bf16[256,8192]{1,0:T(8,128)(2,1)}, bf16[256,8192]{1,0:T(8,128)(2,1)}, u32[]{:S(2)}, u32[]{:S(2)}) collective-permute-start(bf16[256,8192]{1,0:T(8,128)(2,1)} %ao.7), channel_id=1, source_target_pairs={{0,16},{16,0},{32,48},{48,32},{64,80},{80,64},{96,112},{112,96},{1... | collective-permute-start | bytes 12582920 | tf_op jit(solution)/shard_map/ppermute | solution.py:213
  3.0 6.4 %collective-permute-start = (bf16[256,512]{0,1:T(8,128)(2,1)S(1)}, bf16[256,512]{0,1:T(8,128)(2,1)S(1)}, u32[]{:S(2)}, u32[]{:S(2)}) collective-permute-start(bf16[256,512]{0,1:T(8,128)(2,1)S(1)} %copy.3), channel_id=1, source_target_pairs={{0,16},{16,0},{32,48},{48,32},{64,80},{80,64},{96,112},{112,96},{1... | collective-permute-start | bytes 786440 | tf_op jit(solution)/shard_map/ppermute | solution.py:212
  9.4 22.4 %copy-start.2 = (bf16[256,512]{0,1:T(8,128)(2,1)}, bf16[256,512]{0,1:T(8,128)(2,1)S(1)}, u32[]{:S(2)}) copy-start(bf16[256,512]{0,1:T(8,128)(2,1)S(1)} %collective-permute-done) | copy-start | bytes 786436
  9.4 2.3 %copy-start = (bf16[256,8192]{1,0:T(8,128)(2,1)S(1)}, bf16[256,8192]{1,0:T(8,128)(2,1)}, u32[]{:S(2)}) copy-start(bf16[256,8192]{1,0:T(8,128)(2,1)} %ao.7) | copy-start | bytes 12582916
  18.1 28.1 %collective-permute-start.2 = (bf16[528,1024]{1,0:T(8,128)(2,1)}, bf16[528,1024]{1,0:T(8,128)(2,1)S(1)}, u32[]{:S(2)}, u32[]{:S(2)}) collective-permute-start(bf16[528,1024]{1,0:T(8,128)(2,1)} %shard_map.29), channel_id=1, source_target_pairs={{0,64},{16,272},{32,96},{48,304},{64,0},{80,336},{96,32},{112,368}... | collective-permute-start | bytes 3244040 | tf_op jit(solution)/shard_map/ppermute | solution.py:223
  27.8 18.6 %collective-permute-start.3 = (bf16[528,1024]{1,0:T(8,128)(2,1)}, bf16[528,1024]{1,0:T(8,128)(2,1)}, u32[]{:S(2)}, u32[]{:S(2)}) collective-permute-start(bf16[528,1024]{1,0:T(8,128)(2,1)} %shard_map.30), channel_id=1, source_target_pairs={{0,32},{16,144},{32,64},{48,176},{64,96},{80,208},{96,0},{112,240}... | collective-permute-start | bytes 3244040 | tf_op jit(solution)/shard_map/ppermute | solution.py:223
  38.1 18.6 %collective-permute-start.4 = (bf16[528,1024]{1,0:T(8,128)(2,1)}, bf16[528,1024]{1,0:T(8,128)(2,1)}, u32[]{:S(2)}, u32[]{:S(2)}) collective-permute-start(bf16[528,1024]{1,0:T(8,128)(2,1)} %shard_map.31), channel_id=1, source_target_pairs={{0,96},{16,400},{32,0},{48,432},{64,32},{80,464},{96,64},{112,496}... | collective-permute-start | bytes 3244040 | tf_op jit(solution)/shard_map/ppermute | solution.py:223
  40.2 1.0 copy-start.3
  46.2 23.1 %copy-start.1 = (f32[512,1024]{1,0:T(8,128)}, f32[512,1024]{1,0:T(8,128)S(1)}, u32[]{:S(2)}) copy-start(f32[512,1024]{1,0:T(8,128)S(1)} %shard_map.28.own) | copy-start | bytes 6291460
  59.5 14.6 %collective-permute-start.7 = (bf16[528,256]{1,0:T(8,128)(2,1)}, bf16[528,256]{1,0:T(8,128)(2,1)S(1)}, u32[]{:S(2)}, u32[]{:S(2)}) collective-permute-start(bf16[528,256]{1,0:T(8,128)(2,1)} %shard_map.34), channel_id=1, source_target_pairs={{0,384},{16,112},{32,416},{48,16},{64,448},{80,48},{96,480},{112,8... | collective-permute-start | bytes 811016 | tf_op jit(solution)/shard_map/ppermute | solution.py:233
  64.9 9.2 %collective-permute-start.6 = (bf16[528,256]{1,0:T(8,128)(2,1)}, bf16[528,256]{1,0:T(8,128)(2,1)}, u32[]{:S(2)}, u32[]{:S(2)}) collective-permute-start(bf16[528,256]{1,0:T(8,128)(2,1)} %shard_map.33), channel_id=1, source_target_pairs={{0,128},{16,48},{32,160},{48,80},{64,192},{80,112},{96,224},{112,1... | collective-permute-start | bytes 811016 | tf_op jit(solution)/shard_map/ppermute | solution.py:233
  72.1 10.1 %collective-permute-start.5 = (bf16[528,256]{1,0:T(8,128)(2,1)}, bf16[528,256]{1,0:T(8,128)(2,1)S(1)}, u32[]{:S(2)}, u32[]{:S(2)}) collective-permute-start(bf16[528,256]{1,0:T(8,128)(2,1)} %shard_map.32), channel_id=1, source_target_pairs={{0,256},{16,80},{32,288},{48,112},{64,320},{80,16},{96,352},{112,4... | collective-permute-start | bytes 811016 | tf_op jit(solution)/shard_map/ppermute | solution.py:233

commit v2 on v0

v2 whole, which is shorter than its diff:
```python
import functools

import jax
import jax.numpy as jnp
from jax import lax
from jax.experimental import pallas as pl
from jax.experimental.pallas import tpu as pltpu
from jax.sharding import PartitionSpec as P

BLOCK = 128
COLS = 512
NBLK = COLS // BLOCK
PART = 256
NX = 4
NY = 4
TAIL = 16
F32 = jnp.float32
BF16 = jnp.bfloat16
SPAN = 124.0


def to_grid(x):
    return (x + jnp.abs(x) * (2.0**-22)).astype(jnp.float8_e4m3fn).astype(F32)


def quantize(g):
    top = jnp.max(jnp.abs(g), axis=0, keepdims=True)
    scale = ((top + 1e-06) / 448.0).astype(BF16).astype(F32)
    return to_grid(g * (1.0 / scale)), scale


def encode(s):
    top = jnp.max(jnp.abs(s), axis=0, keepdims=True)
    norm = (top * 1.004 + 1e-30).astype(BF16)
    return jnp.exp2(s * (SPAN / norm.astype(F32))).astype(BF16), norm


def decode(code, norm):
    return jnp.log2(code.astype(F32)) * (norm * (1.0 / SPAN))


def rows_of(b):
    return pl.ds(b * BLOCK, BLOCK)


def lanes_of(q):
    return pl.ds(pl.multiple_of(q * PART, PART), PART)


IN_HBM = pl.BlockSpec(memory_space=pltpu.MemorySpace.HBM)
ANY = pl.BlockSpec(memory_space=pl.ANY)
LARGE = pltpu.CompilerParams(vmem_limit_bytes=63 * 2**20 + 2**19)
SMALL = pltpu.CompilerParams(vmem_limit_bytes=24 * 2**20)


def block_sum(g, a, b):
    total = None
    for i in range(g.shape[0]):
        local = lax.dot_general(
            g[i, :, rows_of(b)], a[i], (((0,), (0,)), ((), ())), preferred_element_type=F32
        )
        codes, scale = quantize(local)
        part = codes * scale
        total = part if total is None else total + part
    return total


def put_coded(out, totals):
    norms = []
    for b, total in enumerate(totals):
        code, norm = encode(total)
        out[rows_of(b), :] = code
        norms.append(norm.astype(F32))
    n = norms[0].shape[1]
    out[COLS : COLS + TAIL, :] = jnp.concatenate(
        norms + [jnp.zeros((TAIL - NBLK, n), F32)], axis=0
    ).astype(BF16)


def get_coded(ref, norms, b):
    return decode(ref[rows_of(b), :], norms[b : b + 1, :])


def norms_of(ref):
    return ref[COLS : COLS + TAIL, :].astype(F32)


def position():
    me = lax.axis_index("inner")
    return me // (2 * NX), (me // 2) % NX, me % 2


def part_for(k, q, other=False):
    y, x, c = position()
    c = 1 - c if other else c
    return 2 * jnp.where(c == 0, q * NX + (x + k) % NX, ((y + k) % NY) * NX + q) + c


SWAPPED = (1, 3, 0)


def gather(a, g, buf, in_sem, parts):
    copies = [
        pltpu.make_async_copy(a.at[:, lanes_of(part)], buf.at[:, pl.ds(j * PART, PART)], in_sem.at[j])
        for j, part in enumerate(parts)
    ]
    n = len(parts)
    copies.append(pltpu.make_async_copy(g, buf.at[:, pl.ds(n * PART, COLS)], in_sem.at[n]))
    return copies


def swap_kernel(a, g, out, buf, in_sem, out_sem):
    copies = gather(a, g, buf, in_sem, [part_for(k, q, True) for k in SWAPPED for q in range(4)])
    for copy in copies:
        copy.start()
    for copy in copies:
        copy.wait()
    put = pltpu.make_async_copy(buf, out, out_sem)
    put.start()
    put.wait()


def swap_payload(a, g):
    shape = (a.shape[0], 12 * PART + COLS)
    return pl.pallas_call(
        swap_kernel,
        in_specs=[IN_HBM, ANY],
        out_specs=ANY,
        scratch_shapes=[
            pltpu.VMEM(shape, BF16),
            pltpu.SemaphoreType.DMA((13,)),
            pltpu.SemaphoreType.DMA,
        ],
        out_shape=jax.ShapeDtypeStruct(shape, BF16),
        compiler_params=LARGE,
    )(a, g)


def far_kernel(a, g, after, same, cross, buf, in_sem, out_sem):
    copies = [
        gather(a, g, buf.at[i], in_sem.at[i], [part_for(2, q, i == 1) for q in range(4)]) for i in range(2)
    ]
    puts = [pltpu.make_async_copy(buf.at[i], (same, cross)[i], out_sem.at[i]) for i in range(2)]
    for i in range(2):
        for copy in copies[i]:
            copy.start()
    for i in range(2):
        for copy in copies[i]:
            copy.wait()
        puts[i].start()
    for put in puts:
        put.wait()


def far_payloads(a, g, after):
    shape = (a.shape[0], 4 * PART + COLS)
    return pl.pallas_call(
        far_kernel,
        in_specs=[IN_HBM, ANY, ANY],
        out_specs=[ANY, ANY],
        scratch_shapes=[
            pltpu.VMEM((2,) + shape, BF16),
            pltpu.SemaphoreType.DMA((2, 5)),
            pltpu.SemaphoreType.DMA((2,)),
        ],
        out_shape=[jax.ShapeDtypeStruct(shape, BF16)] * 2,
        compiler_params=LARGE,
    )(a, g, after)


def sums_kernel(ks, kept, g_own, a_own, swapped, *rest):
    n, far = len(ks), rest[: 2 * kept]
    outs, (gbuf, abuf, obuf, gsem, asem, osem) = rest[2 * kept : 2 * kept + n], rest[2 * kept + n :]
    devices = 2 + len(far)

    def g_in(i):
        if i == 0:
            src = g_own
        else:
            src = swapped.at[:, 12 * PART :] if i == 1 else far[i - 2].at[:, 4 * PART :]
        return pltpu.make_async_copy(src, gbuf.at[i], gsem.at[i])

    def a_in(m, q, i):
        if i == 0:
            src = a_own.at[:, lanes_of(part_for(ks[m], q))]
        elif i == 1:
            src = swapped.at[:, lanes_of(4 * SWAPPED.index(ks[m]) + q)]
        else:
            src = far[i - 2].at[:, lanes_of(q)]
        return pltpu.make_async_copy(src, abuf.at[4 * m + q, i], asem.at[4 * m + q, i])

    def put(m, q):
        return pltpu.make_async_copy(obuf.at[4 * m + q], outs[m].at[:, lanes_of(q)], osem.at[4 * m + q])

    for i in range(devices):
        g_in(i).start()
        a_in(0, 0, i).start()
    for j in range(1, 4 * n):
        for i in range(devices):
            a_in(j // 4, j % 4, i).start()
    for i in range(devices):
        g_in(i).wait()
    for m in range(n):

        def step(q, carry):
            j = 4 * m + q
            for i in range(devices):
                a_in(m, q, i).wait()
            if kept:
                for b in range(NBLK):
                    obuf[j, rows_of(b), :] = block_sum(gbuf, abuf.at[j], b)
            else:
                put_coded(obuf.at[j], [block_sum(gbuf, abuf.at[j], b) for b in range(NBLK)])
            put(m, q).start()
            return carry

        lax.fori_loop(0, 4, step, 0)
    for m in range(n):
        for q in range(4):
            put(m, q).wait()


def sums(ks, g_own, a_own, swapped, far=()):
    n, tok, kept = len(ks), a_own.shape[0], len(far) > 0
    devices = 2 + len(far)
    height, dtype = (COLS, F32) if kept else (COLS + TAIL, BF16)
    return pl.pallas_call(
        functools.partial(sums_kernel, ks, kept),
        in_specs=[ANY, IN_HBM, ANY] + [ANY] * len(far),
        out_specs=[ANY] * n,
        scratch_shapes=[
            pltpu.VMEM((devices, tok, COLS), BF16),
            pltpu.VMEM((4 * n, devices, tok, PART), BF16),
            pltpu.VMEM((4 * n, height, PART), dtype),
            pltpu.SemaphoreType.DMA((devices,)),
            pltpu.SemaphoreType.DMA((4 * n, devices)),
            pltpu.SemaphoreType.DMA((4 * n,)),
        ],
        out_shape=[jax.ShapeDtypeStruct((height, 4 * PART), dtype)] * n,
        compiler_params=LARGE,
        cost_estimate=pl.CostEstimate(
            flops=2 ** (36 if kept else 31), bytes_accessed=2**20, transcendentals=0
        ),
    )(g_own, a_own, swapped, *far)


def row_sum_kernel(own, r0, r1, out, fbuf, rbuf, obuf, fsem, rsem, osem):
    def f_in(q):
        return pltpu.make_async_copy(own.at[:, lanes_of(q)], fbuf.at[q], fsem.at[q])

    def r_in(q, i):
        return pltpu.make_async_copy((r0, r1)[i].at[:, lanes_of(q)], rbuf.at[q, i], rsem.at[q, i])

    def put(q):
        return pltpu.make_async_copy(obuf.at[q], out.at[q], osem.at[q])

    for q in range(4):
        f_in(q).start()
        for i in range(2):
            r_in(q, i).start()

    def step(q, carry):
        f_in(q).wait()
        for i in range(2):
            r_in(q, i).wait()
        norms = [norms_of(rbuf.at[q, i]) for i in range(2)]
        totals = []
        for b in range(NBLK):
            total = fbuf[q, rows_of(b), :]
            for i in range(2):
                total = total + get_coded(rbuf.at[q, i], norms[i], b)
            totals.append(total)
        put_coded(obuf.at[q], totals)
        put(q).start()
        return carry

    lax.fori_loop(0, 4, step, 0)
    for q in range(4):
        put(q).wait()


def row_sum(own, r0, r1):
    return pl.pallas_call(
        row_sum_kernel,
        in_specs=[ANY] * 3,
        out_specs=ANY,
        out_shape=jax.ShapeDtypeStruct((4, COLS + TAIL, PART), BF16),
        scratch_shapes=[
            pltpu.VMEM((4, COLS, PART), F32),
            pltpu.VMEM((4, 2, COLS + TAIL, PART), BF16),
            pltpu.VMEM((4, COLS + TAIL, PART), BF16),
            pltpu.SemaphoreType.DMA((4,)),
            pltpu.SemaphoreType.DMA((4, 2)),
            pltpu.SemaphoreType.DMA((4,)),
        ],
        compiler_params=LARGE,
    )(own, r0, r1)


def group_kernel(got, out):
    n = got.shape[2]
    n_outer = out.shape[0]
    rows = n // n_outer
    norms = [norms_of(got.at[s]) for s in range(4)]
    for b in range(NBLK):
        total = get_coded(got.at[0], norms[0], b)
        for s in range(1, 4):
            total = total + get_coded(got.at[s], norms[s], b)
        codes, scale = quantize(total)
        sent = (codes * scale).T.astype(BF16)
        out[:, b * rows : (b + 1) * rows, :] = sent.reshape(n_outer, rows, BLOCK)


def group_sent(got, n_outer):
    return pl.pallas_call(
        group_kernel,
        out_shape=jax.ShapeDtypeStruct((n_outer, NBLK * (PART // n_outer), BLOCK), BF16),
        compiler_params=SMALL,
    )(got)


def final_kernel(got, out):
    rows = out.shape[0]
    for b in range(NBLK):
        total = jnp.zeros((rows, BLOCK), F32)
        for s in range(got.shape[0]):
            total = total + got[s, b * rows : (b + 1) * rows, :].astype(F32)
        out[:, b * BLOCK : (b + 1) * BLOCK] = total


def final_sum(got):
    rows = got.shape[1] // NBLK
    return pl.pallas_call(
        final_kernel,
        out_shape=jax.ShapeDtypeStruct((rows, COLS), F32),
        compiler_params=SMALL,
    )(got)


def index_of(y, x, c):
    return ((y % NY) * NX + x % NX) * 2 + c


def ring(k, cross=False):
    pairs = []
    for y in range(NY):
        for x in range(NX):
            pairs.append((index_of(y, x, int(cross)), index_of(y, x + k, 0)))
            pairs.append((index_of(y, x, 1 - int(cross)), index_of(y + k, x, 1)))
    return pairs


def columns():
    return [[index_of(y, x, 0) for y in range(NY)] for x in range(NX)] + [
        [index_of(y, x, 1) for x in range(NX)] for y in range(NY)
    ]


def shards(activations, output_grads):
    n_outer = lax.axis_size("outer")
    swap = [(i, i ^ 1) for i in range(2 * NX * NY)]
    to_swap = swap_payload(activations, output_grads)
    swapped = lax.ppermute(to_swap, "inner", swap)
    same, cross = far_payloads(activations, output_grads, to_swap)
    far = (lax.ppermute(same, "inner", ring(2)), lax.ppermute(cross, "inner", ring(2, cross=True)))
    ahead, behind = sums((1, 3), output_grads, activations, swapped)
    got_ahead = lax.ppermute(ahead, "inner", ring(1))
    got_behind = lax.ppermute(behind, "inner", ring(3))
    (own,) = sums((0,), output_grads, activations, swapped, far)
    coded = row_sum(own, got_ahead, got_behind)
    got = lax.all_to_all(
        coded, "inner", split_axis=0, concat_axis=0, tiled=True, axis_index_groups=columns()
    )
    packed = group_sent(got, n_outer)
    return final_sum(lax.all_to_all(packed, "outer", split_axis=0, concat_axis=0, tiled=True))


def solution(mesh):
    return jax.shard_map(
        shards,
        mesh=mesh,
        in_specs=(P(("inner", "outer"), None), P(("inner", "outer"), None)),
        out_specs=P(("inner", "outer"), None),
        check_vma=False,
    )
```

time: 279 us -> 96.4 us (0.35)
  waiting for transfers between devices: 128 us -> 7.1 us
  other arithmetic: 74 us -> 0 us
  blocking collectives: 0 us -> 48.2 us
  local copies, waits for them, and re-layouts: 30.8 us -> 0 us
  Pallas kernels: 0 us -> 24.4 us
  starting transfers between devices: 34.7 us -> 16.1 us
  matrix products: 10.3 us -> 0 us
    all_to_all x4 -> x0, waiting for transfers between devices: 128 us -> none  [the longest x1 103 us: shards(): lax.all_to_all(codes, 'inner', split_axis=0, concat_axis=0, tiled=True)]
    all_to_all x0 -> x2, blocking collectives: none -> 48.2 us  [the longest x1 32.7 us: shards(): lax.all_to_all(packed, 'outer', split_axis=0, concat_axis=0, tiled=True)]
    convert_element_type x7 -> x0, other arithmetic: 47.3 us -> none  [the longest x2 47.3 us: quantize(): codes = to_grid(blocks / widened[..., None]).astype(jnp.bfloat16)]
    all_to_all x4 -> x0, starting transfers between devices: 34.7 us -> none  [the longest x1 15.2 us: shards(): lax.all_to_all(scale2, 'outer', split_axis=0, concat_axis=0, tiled=True)]
    pallas_call x0 -> x7, Pallas kernels: none -> 24.4 us  [the longest x2 14.4 us: sums(): pl.pallas_call(functools.partial(sums_kernel, ks, kept), in_specs=[ANY, I...]
    reshape x2 -> x0, local copies, waits for them, and re-layouts: 19.9 us -> none  [the longest x1 19.2 us: shards(): codes, scale = quantize(local.reshape(n_inner, own_rows, n_blocks, BLOCK))]
    ppermute x0 -> x5, starting transfers between devices: none -> 16.1 us  [the longest x1 4.93 us: shards(): lax.ppermute(same, 'inner', ring(2))]
    reduce_max x2 -> x0, other arithmetic: 14.8 us -> none  [quantize(): jnp.max(jnp.abs(blocks), axis=-1) + 1e-06]
  transfers between devices with their start and end apart: 4 -> 5, of which waited for: 3 -> 3; matrix products, arithmetic and copies ran while one was open for 19% -> 0% of each run, Pallas kernels for 0% -> 18%
where the time goes in v2:
time: 96.4 us; the launch traced here: 95.9 us
  blocking collectives  48.2 us (50%)
  Pallas kernels  24.4 us (25%)
  starting transfers between devices  16.1 us (17%)
  waiting for transfers between devices  7.1 us (7%)
    all_to_all x1, blocking collectives, shards(): lax.all_to_all(packed, 'outer', split_axis=0, concat_axis=0, tiled=True)  32.7 us
    all_to_all x1, blocking collectives, shards(): lax.all_to_all(coded, 'inner', split_axis=0, concat_axis=0, tiled=True, a...  15.5 us
    pallas_call x2, Pallas kernels, sums(): pl.pallas_call(functools.partial(sums_kernel, ks, kept), in_specs=[ANY, I...  14.4 us
    ppermute x1, starting transfers between devices, shards(): lax.ppermute(same, 'inner', ring(2))  4.93 us
    ppermute x1, starting transfers between devices, shards(): got_behind = lax.ppermute(behind, 'inner', ring(3))  3.66 us
    ppermute x1, waiting for transfers between devices, shards(): got_ahead = lax.ppermute(ahead, 'inner', ring(1))  3.64 us
    ppermute x1, starting transfers between devices, shards(): got_ahead = lax.ppermute(ahead, 'inner', ring(1))  3.4 us
    ppermute x1, waiting for transfers between devices, shards(): lax.ppermute(cross, 'inner', ring(2, cross=True))  3.37 us
  transfers between devices with their start and end apart: 5, of which 3 were waited for; matrix products, arithmetic and copies ran while one was open for 0% of the time, Pallas kernels for 18%

profile of v2, /device:TPU:32, one launch (start us, length us, event | category | flops | bytes accessed | tf_op | source)
XLA Modules:
  0.0 95.9 jit_solution(4263258460758297971)
XLA Ops:
  0.0 2.9 %shard_map.28.after = bf16[256,3584]{1,0:T(8,128)(2,1)} custom-call(bf16[256,8192]{1,0:T(8,128)(2,1)} %a_own.3, bf16[256,512]{1,0:T(8,128)(2,1)} %g_own.3), custom_call_target="tpu_custom_call" | custom-call | tf_op jit(solution)/shard_map/pallas_call | solution.py:125
  2.9 1.9 %collective-permute-start = (bf16[256,3584]{1,0:T(8,128)(2,1)}, bf16[256,3584]{1,0:T(8,128)(2,1)}, u32[]{:S(2)}, u32[]{:S(2)}) collective-permute-start(bf16[256,3584]{1,0:T(8,128)(2,1)} %shard_map.28.after), channel_id=1, source_target_pairs={{0,16},{16,0},{32,48},{48,32},{64,80},{80,64},{96,112},{112,96},{1... | collective-permute-start | bytes 5505032 | tf_op jit(solution)/shard_map/ppermute | solution.py:363
  4.8 2.6 %shard_map.29 = (bf16[256,1536]{1,0:T(8,128)(2,1)}, bf16[256,1536]{1,0:T(8,128)(2,1)}) custom-call(bf16[256,8192]{1,0:T(8,128)(2,1)} %a_own.3, bf16[256,512]{1,0:T(8,128)(2,1)} %g_own.3, bf16[256,3584]{1,0:T(8,128)(2,1)} %shard_map.28.after), custom_call_target="tpu_custom_call" | custom-call | tf_op jit(solution)/shard_map/pallas_call | solution.py:157
  7.4 4.9 %collective-permute-start.1 = (bf16[256,1536]{1,0:T(8,128)(2,1)}, bf16[256,1536]{1,0:T(8,128)(2,1)}, u32[]{:S(2)}, u32[]{:S(2)}) collective-permute-start(bf16[256,1536]{1,0:T(8,128)(2,1)} %get-tuple-element.9), channel_id=1, source_target_pairs={{0,64},{16,272},{32,96},{48,304},{64,0},{80,336},{96,32},{112,368}... | collective-permute-start | bytes 2359304 | tf_op jit(solution)/shard_map/ppermute | solution.py:365
  12.4 2.2 %collective-permute-start.2 = (bf16[256,1536]{1,0:T(8,128)(2,1)}, bf16[256,1536]{1,0:T(8,128)(2,1)}, u32[]{:S(2)}, u32[]{:S(2)}) collective-permute-start(bf16[256,1536]{1,0:T(8,128)(2,1)} %get-tuple-element.10), channel_id=1, source_target_pairs={{16,64},{0,272},{48,96},{32,304},{80,0},{64,336},{112,32},{96,368}... | collective-permute-start | bytes 2359304 | tf_op jit(solution)/shard_map/ppermute | solution.py:365
  14.6 0.0 collective-permute-done.swapped
  14.6 7.8 %shard_map.31 = (bf16[528,1024]{1,0:T(8,128)(2,1)}, bf16[528,1024]{1,0:T(8,128)(2,1)}) custom-call(bf16[256,512]{1,0:T(8,128)(2,1)} %g_own.3, bf16[256,8192]{1,0:T(8,128)(2,1)} %a_own.3, bf16[256,3584]{1,0:T(8,128)(2,1)} %collective-permute-done.swapped), custom_call_target="tpu_custom_call" | custom-call | flops 2147483648 | bytes 1048576 | tf_op jit(solution)/shard_map/pallas_call | solution.py:227
  22.5 3.4 %collective-permute-start.3 = (bf16[528,1024]{1,0:T(8,128)(2,1)}, bf16[528,1024]{1,0:T(8,128)(2,1)}, u32[]{:S(2)}, u32[]{:S(2)}) collective-permute-start(bf16[528,1024]{1,0:T(8,128)(2,1)} %get-tuple-element.11), channel_id=1, source_target_pairs={{0,32},{16,144},{32,64},{48,176},{64,96},{80,208},{96,0},{112,240}... | collective-permute-start | bytes 3244040 | tf_op jit(solution)/shard_map/ppermute | solution.py:367
  25.9 3.7 %collective-permute-start.4 = (bf16[528,1024]{1,0:T(8,128)(2,1)}, bf16[528,1024]{1,0:T(8,128)(2,1)}, u32[]{:S(2)}, u32[]{:S(2)}) collective-permute-start(bf16[528,1024]{1,0:T(8,128)(2,1)} %get-tuple-element.12), channel_id=1, source_target_pairs={{0,96},{16,400},{32,0},{48,432},{64,32},{80,464},{96,64},{112,496}... | collective-permute-start | bytes 3244040 | tf_op jit(solution)/shard_map/ppermute | solution.py:368
  29.5 0.0 collective-permute-done.1.rest_0_
  29.5 3.4 %collective-permute-done.2.rest_1_ = bf16[256,1536]{1,0:T(8,128)(2,1)} collective-permute-done((bf16[256,1536]{1,0:T(8,128)(2,1)}, bf16[256,1536]{1,0:T(8,128)(2,1)}, u32[]{:S(2)}, u32[]{:S(2)}) %collective-permute-start.2) | collective-permute-done | bytes 786464 | tf_op jit(solution)/shard_map/ppermute | solution.py:365
  32.9 6.6 %shard_map.30.own = f32[512,1024]{1,0:T(8,128)} custom-call(bf16[256,512]{1,0:T(8,128)(2,1)} %g_own.3, bf16[256,8192]{1,0:T(8,128)(2,1)} %a_own.3, bf16[256,3584]{1,0:T(8,128)(2,1)} %collective-permute-done.swapped, bf16[256,1536]{1,0:T(8,128)(2,1)} %collective-permute-done.1.rest_0_, bf16[256,1536]{1,0:T(8,128)(2,1)} %collective-permute-done.2.rest_1_), custom_call_target="tpu_custom_call" | custom-call | flops 68719476736 | bytes 1048576 | tf_op jit(solution)/shard_map/pallas_call | solution.py:227
  39.5 3.6 %collective-permute-done.3.r0 = bf16[528,1024]{1,0:T(8,128)(2,1)} collective-permute-done((bf16[528,1024]{1,0:T(8,128)(2,1)}, bf16[528,1024]{1,0:T(8,128)(2,1)}, u32[]{:S(2)}, u32[]{:S(2)}) %collective-permute-start.3) | collective-permute-done | bytes 1081376 | tf_op jit(solution)/shard_map/ppermute | solution.py:367
  43.2 0.1 collective-permute-done.4.r1
  43.2 3.3 %shard_map.32 = bf16[4,528,256]{2,1,0:T(8,128)(2,1)} custom-call(f32[512,1024]{1,0:T(8,128)} %shard_map.30.own, bf16[528,1024]{1,0:T(8,128)(2,1)} %collective-permute-done.3.r0, bf16[528,1024]{1,0:T(8,128)(2,1)} %collective-permute-done.4.r1), custom_call_target="tpu_custom_call" | custom-call | tf_op jit(solution)/shard_map/pallas_call | solution.py:283
  46.5 15.5 %all_to_all.10.got = bf16[4,528,256]{2,1,0:T(8,128)(2,1)S(1)} all-to-all(bf16[4,528,256]{2,1,0:T(8,128)(2,1)} %shard_map.32), channel_id=1, replica_groups={{0,128,256,384},{32,160,288,416},{64,192,320,448},{96,224,352,480},{16,..., dimensions={0} | all-to-all | bytes 2162688 | tf_op jit(solution)/shard_map/all_to_all | solution.py:371
  62.1 0.5 shard_map.33
  62.6 32.7 %all_to_all.11.got = bf16[16,64,128]{2,1,0:T(8,128)(2,1)S(1)} all-to-all(bf16[16,64,128]{2,1,0:T(8,128)(2,1)S(1)} %shard_map.33), channel_id=1, replica_groups=mesh['inner'=32,'outer'=16] {'outer'}, dimensions={0} | all-to-all | bytes 524288 | tf_op jit(solution)/shard_map/all_to_all | solution.py:375
  95.3 0.7 shard_map.34
Async XLA Ops:
  2.9 11.7 %collective-permute-start = (bf16[256,3584]{1,0:T(8,128)(2,1)}, bf16[256,3584]{1,0:T(8,128)(2,1)}, u32[]{:S(2)}, u32[]{:S(2)}) collective-permute-start(bf16[256,3584]{1,0:T(8,128)(2,1)} %shard_map.28.after), channel_id=1, source_target_pairs={{0,16},{16,0},{32,48},{48,32},{64,80},{80,64},{96,112},{112,96},{1... | collective-permute-start | bytes 5505032 | tf_op jit(solution)/shard_map/ppermute | solution.py:363
  7.4 22.1 %collective-permute-start.1 = (bf16[256,1536]{1,0:T(8,128)(2,1)}, bf16[256,1536]{1,0:T(8,128)(2,1)}, u32[]{:S(2)}, u32[]{:S(2)}) collective-permute-start(bf16[256,1536]{1,0:T(8,128)(2,1)} %get-tuple-element.9), channel_id=1, source_target_pairs={{0,64},{16,272},{32,96},{48,304},{64,0},{80,336},{96,32},{112,368}... | collective-permute-start | bytes 2359304 | tf_op jit(solution)/shard_map/ppermute | solution.py:365
  12.4 20.5 %collective-permute-start.2 = (bf16[256,1536]{1,0:T(8,128)(2,1)}, bf16[256,1536]{1,0:T(8,128)(2,1)}, u32[]{:S(2)}, u32[]{:S(2)}) collective-permute-start(bf16[256,1536]{1,0:T(8,128)(2,1)} %get-tuple-element.10), channel_id=1, source_target_pairs={{16,64},{0,272},{48,96},{32,304},{80,0},{64,336},{112,32},{96,368}... | collective-permute-start | bytes 2359304 | tf_op jit(solution)/shard_map/ppermute | solution.py:365
  22.5 20.7 %collective-permute-start.3 = (bf16[528,1024]{1,0:T(8,128)(2,1)}, bf16[528,1024]{1,0:T(8,128)(2,1)}, u32[]{:S(2)}, u32[]{:S(2)}) collective-permute-start(bf16[528,1024]{1,0:T(8,128)(2,1)} %get-tuple-element.11), channel_id=1, source_target_pairs={{0,32},{16,144},{32,64},{48,176},{64,96},{80,208},{96,0},{112,240}... | collective-permute-start | bytes 3244040 | tf_op jit(solution)/shard_map/ppermute | solution.py:367
  25.9 17.4 %collective-permute-start.4 = (bf16[528,1024]{1,0:T(8,128)(2,1)}, bf16[528,1024]{1,0:T(8,128)(2,1)}, u32[]{:S(2)}, u32[]{:S(2)}) collective-permute-start(bf16[528,1024]{1,0:T(8,128)(2,1)} %get-tuple-element.12), channel_id=1, source_target_pairs={{0,96},{16,400},{32,0},{48,432},{64,32},{80,464},{96,64},{112,496}... | collective-permute-start | bytes 3244040 | tf_op jit(solution)/shard_map/ppermute | solution.py:368

commit v3 on v2

v3 whole, which is shorter than its diff:
```python
import functools

import jax
import jax.numpy as jnp
from jax import lax
from jax.experimental import pallas as pl
from jax.experimental.pallas import tpu as pltpu
from jax.sharding import PartitionSpec as P

BLOCK = 128
COLS = 512
NBLK = COLS // BLOCK
PART = 256
NX = 4
NY = 4
TAIL = 16
F32 = jnp.float32
BF16 = jnp.bfloat16
SPAN = 124.0


def to_grid(x):
    return (x + jnp.abs(x) * (2.0**-22)).astype(jnp.float8_e4m3fn).astype(F32)


def quantize(g):
    top = jnp.max(jnp.abs(g), axis=0, keepdims=True)
    scale = ((top + 1e-06) / 448.0).astype(BF16).astype(F32)
    return to_grid(g * (1.0 / scale)), scale


def encode(s):
    top = jnp.max(jnp.abs(s), axis=0, keepdims=True)
    norm = (top * 1.004 + 1e-30).astype(BF16)
    return jnp.exp2(s * (SPAN / norm.astype(F32))).astype(BF16), norm


def decode(code, norm):
    return jnp.log2(code.astype(F32)) * (norm * (1.0 / SPAN))


def rows_of(b):
    return pl.ds(b * BLOCK, BLOCK)


def lanes_of(q):
    return pl.ds(pl.multiple_of(q * PART, PART), PART)


HBM, VMEM = pltpu.MemorySpace.HBM, pltpu.MemorySpace.VMEM
ANY, WHOLE = pl.BlockSpec(memory_space=pl.ANY), pl.BlockSpec(memory_space=VMEM)
PARAMS = pltpu.CompilerParams(vmem_limit_bytes=24 * 2**20)


def near(*arrays):
    return [pltpu.with_memory_space_constraint(x, VMEM) for x in arrays]


def block_sum(local, b):
    total = None
    for i in range(local.shape[0]):
        codes, scale = quantize(local[i, rows_of(b), :])
        part = codes * scale
        total = part if total is None else total + part
    return total


def put_coded(out, lanes, totals):
    norms = []
    for b, total in enumerate(totals):
        code, norm = encode(total)
        out[rows_of(b), lanes] = code
        norms.append(norm.astype(F32))
    n = norms[0].shape[1]
    out[COLS : COLS + TAIL, lanes] = jnp.concatenate(
        norms + [jnp.zeros((TAIL - NBLK, n), F32)], axis=0
    ).astype(BF16)


def norms_of(ref, lanes):
    return ref[COLS : COLS + TAIL, lanes].astype(F32)


def get_coded(ref, lanes, norms, b):
    return decode(ref[rows_of(b), lanes], norms[b : b + 1, :])


def position():
    me = lax.axis_index("inner")
    return me // (2 * NX), (me // 2) % NX, me % 2


def part_for(k, q, other=False):
    y, x, c = position()
    c = 1 - c if other else c
    return 2 * jnp.where(c == 0, q * NX + (x + k) % NX, ((y + k) % NY) * NX + q) + c


SWAPPED = (1, 3, 0)


def send_kernel(a, g, *rest):
    outs, sems = rest[:3], rest[3:]
    parts = [
        [part_for(k, q, True) for k in SWAPPED for q in range(4)],
        [part_for(2, q) for q in range(4)],
        [part_for(2, q, True) for q in range(4)],
    ]
    copies = []
    for out, sem, group in zip(outs, sems, parts):
        n = len(group)
        for j, p in enumerate(group):
            copies.append(
                pltpu.make_async_copy(a.at[:, lanes_of(p)], out.at[:, pl.ds(j * PART, PART)], sem.at[j])
            )
        copies.append(pltpu.make_async_copy(g, out.at[:, pl.ds(n * PART, COLS)], sem.at[n]))
    for copy in copies:
        copy.start()
    for copy in copies:
        copy.wait()


def to_send(a, g):
    tok = a.shape[0]
    shapes = [(tok, 12 * PART + COLS)] + [(tok, 4 * PART + COLS)] * 2
    return pl.pallas_call(
        send_kernel,
        in_specs=[ANY, ANY],
        out_specs=[WHOLE] * 3,
        scratch_shapes=[pltpu.SemaphoreType.DMA((n,)) for n in (13, 5, 5)],
        out_shape=[pltpu.VMEM(shape, BF16) for shape in shapes],
        compiler_params=PARAMS,
    )(*[pltpu.with_memory_space_constraint(x, HBM) for x in (a, g)])


def sums_kernel(ks, kept, g_own, a_own, swapped, *rest):
    n = len(ks)
    far, outs, (abuf, gt, local, asem) = rest[: 2 * kept], rest[2 * kept : 2 * kept + n], rest[2 * kept + n :]
    devices = 2 + len(far)

    def a_in(m, q):
        src = a_own.at[:, lanes_of(part_for(ks[m], q))]
        return pltpu.make_async_copy(src, abuf.at[4 * m + q], asem.at[4 * m + q])

    for j in range(4 * n):
        a_in(j // 4, j % 4).start()
    gt[0] = g_own[...].T
    gt[1] = swapped[:, 12 * PART :].T
    for i, other in enumerate(far):
        gt[2 + i] = other[:, 4 * PART :].T
    for m in range(n):

        def step(q, carry):
            lanes = lanes_of(q)
            a_in(m, q).wait()
            columns = [abuf[4 * m + q], swapped[:, lanes_of(4 * SWAPPED.index(ks[m]) + q)]]
            columns += [other[:, lanes] for other in far]
            for i in range(devices):
                local[i] = jnp.dot(gt[i], columns[i], preferred_element_type=F32)
            if kept:
                for b in range(NBLK):
                    outs[0][rows_of(b), lanes] = block_sum(local, b)
            else:
                put_coded(outs[m], lanes, [block_sum(local, b) for b in range(NBLK)])
            return carry

        lax.fori_loop(0, 4, step, 0)


def sums(ks, g_own, a_own, swapped, far=()):
    n, tok, kept = len(ks), a_own.shape[0], len(far) > 0
    devices = 2 + len(far)
    height, dtype = (COLS, F32) if kept else (COLS + TAIL, BF16)
    return pl.pallas_call(
        functools.partial(sums_kernel, ks, kept),
        in_specs=[WHOLE, ANY, WHOLE] + [WHOLE] * len(far),
        out_specs=[WHOLE] * n,
        scratch_shapes=[
            pltpu.VMEM((4 * n, tok, PART), BF16),
            pltpu.VMEM((devices, COLS, tok), BF16),
            pltpu.VMEM((devices, COLS, PART), F32),
            pltpu.SemaphoreType.DMA((4 * n,)),
        ],
        out_shape=[pltpu.VMEM((height, 4 * PART), dtype)] * n,
        compiler_params=PARAMS,
        cost_estimate=pl.CostEstimate(
            flops=2 ** (36 if kept else 31), bytes_accessed=2**20, transcendentals=0
        ),
    )(*near(g_own), pltpu.with_memory_space_constraint(a_own, HBM), *near(swapped, *far))


def row_sum_kernel(own, r0, r1, out):
    def step(q, carry):
        lanes = lanes_of(q)
        norms = [norms_of(r, lanes) for r in (r0, r1)]
        totals = []
        for b in range(NBLK):
            total = own[rows_of(b), lanes]
            for i, r in enumerate((r0, r1)):
                total = total + get_coded(r, lanes, norms[i], b)
            totals.append(total)
        put_coded(out.at[q], slice(None), totals)
        return carry

    lax.fori_loop(0, 4, step, 0)


def row_sum(own, r0, r1):
    return pl.pallas_call(
        row_sum_kernel,
        in_specs=[WHOLE] * 3,
        out_specs=WHOLE,
        out_shape=pltpu.VMEM((4, COLS + TAIL, PART), BF16),
        compiler_params=PARAMS,
    )(*near(own, r0, r1))


def group_kernel(got, out):
    n = got.shape[2]
    n_outer = out.shape[0]
    rows = n // n_outer
    lanes = slice(None)
    norms = [norms_of(got.at[s], lanes) for s in range(4)]
    for b in range(NBLK):
        total = get_coded(got.at[0], lanes, norms[0], b)
        for s in range(1, 4):
            total = total + get_coded(got.at[s], lanes, norms[s], b)
        codes, scale = quantize(total)
        sent = (codes * scale).T.astype(BF16)
        out[:, b * rows : (b + 1) * rows, :] = sent.reshape(n_outer, rows, BLOCK)


def group_sent(got, n_outer):
    return pl.pallas_call(
        group_kernel,
        in_specs=[WHOLE],
        out_specs=WHOLE,
        out_shape=pltpu.VMEM((n_outer, NBLK * (PART // n_outer), BLOCK), BF16),
        compiler_params=PARAMS,
    )(*near(got))


def final_kernel(got, out):
    rows = out.shape[0]
    for b in range(NBLK):
        total = jnp.zeros((rows, BLOCK), F32)
        for s in range(got.shape[0]):
            total = total + got[s, b * rows : (b + 1) * rows, :].astype(F32)
        out[:, b * BLOCK : (b + 1) * BLOCK] = total


def final_sum(got):
    rows = got.shape[1] // NBLK
    return pl.pallas_call(
        final_kernel,
        out_shape=jax.ShapeDtypeStruct((rows, COLS), F32),
        compiler_params=PARAMS,
    )(*near(got))


def index_of(y, x, c):
    return ((y % NY) * NX + x % NX) * 2 + c


def ring(k, cross=False):
    pairs = []
    for y in range(NY):
        for x in range(NX):
            pairs.append((index_of(y, x, int(cross)), index_of(y, x + k, 0)))
            pairs.append((index_of(y, x, 1 - int(cross)), index_of(y + k, x, 1)))
    return pairs


def columns():
    return [[index_of(y, x, 0) for y in range(NY)] for x in range(NX)] + [
        [index_of(y, x, 1) for x in range(NX)] for y in range(NY)
    ]


def shards(activations, output_grads):
    n_outer = lax.axis_size("outer")
    swap = [(i, i ^ 1) for i in range(2 * NX * NY)]
    to_swap, same, cross = to_send(activations, output_grads)
    swapped = lax.ppermute(to_swap, "inner", swap)
    far = (lax.ppermute(same, "inner", ring(2)), lax.ppermute(cross, "inner", ring(2, cross=True)))
    ahead, behind = sums((1, 3), output_grads, activations, swapped)
    got_ahead = lax.ppermute(ahead, "inner", ring(1))
    got_behind = lax.ppermute(behind, "inner", ring(3))
    (own,) = sums((0,), output_grads, activations, swapped, far)
    coded = row_sum(own, got_ahead, got_behind)
    got = lax.all_to_all(
        coded, "inner", split_axis=0, concat_axis=0, tiled=True, axis_index_groups=columns()
    )
    packed = group_sent(got, n_outer)
    return final_sum(lax.all_to_all(packed, "outer", split_axis=0, concat_axis=0, tiled=True))


def solution(mesh):
    return jax.shard_map(
        shards,
        mesh=mesh,
        in_specs=(P(("inner", "outer"), None), P(("inner", "outer"), None)),
        out_specs=P(("inner", "outer"), None),
        check_vma=False,
    )
```

time: 96.4 us -> 90.3 us (0.937)
  Pallas kernels: 24.4 us -> 14.8 us
  waiting for transfers between devices: 7.1 us -> 10.9 us
    pallas_call x6 -> x5, Pallas kernels: 23.7 us -> 14.2 us  [the longest x2 10.3 us: sums(): pl.pallas_call(functools.partial(sums_kernel, ks, kept), in_specs=[WHOLE,...]
    ppermute x1, waiting for transfers between devices: 3.37 us -> 6.04 us  [shards(): lax.ppermute(cross, 'inner', ring(2, cross=True))]
    ppermute x1, waiting for transfers between devices: 0.01 us -> 1.02 us  [shards(): lax.ppermute(same, 'inner', ring(2))]
  transfers between devices with their start and end apart: 5 -> 5, of which waited for: 3 -> 4; matrix products, arithmetic and copies ran while one was open for 0% -> 0% of each run, Pallas kernels for 18% -> 11%
where the time goes in v3:
time: 90.3 us; the launch traced here: 89.9 us
  blocking collectives  48 us (53%)
  starting transfers between devices  16.1 us (18%)
  Pallas kernels  14.8 us (16%)
  waiting for transfers between devices  10.9 us (12%)
    all_to_all x1, blocking collectives, shards(): lax.all_to_all(packed, 'outer', split_axis=0, concat_axis=0, tiled=True)  32.7 us
    all_to_all x1, blocking collectives, shards(): lax.all_to_all(coded, 'inner', split_axis=0, concat_axis=0, tiled=True, a...  15.3 us
    pallas_call x2, Pallas kernels, sums(): pl.pallas_call(functools.partial(sums_kernel, ks, kept), in_specs=[WHOLE,...  10.3 us
    ppermute x1, waiting for transfers between devices, shards(): lax.ppermute(cross, 'inner', ring(2, cross=True))  6.04 us
    ppermute x1, starting transfers between devices, shards(): lax.ppermute(same, 'inner', ring(2))  4.93 us
    ppermute x1, waiting for transfers between devices, shards(): got_ahead = lax.ppermute(ahead, 'inner', ring(1))  3.73 us
    ppermute x1, starting transfers between devices, shards(): got_behind = lax.ppermute(behind, 'inner', ring(3))  3.65 us
    ppermute x1, starting transfers between devices, shards(): got_ahead = lax.ppermute(ahead, 'inner', ring(1))  3.4 us
  transfers between devices with their start and end apart: 5, of which 4 were waited for; matrix products, arithmetic and copies ran while one was open for 0% of the time, Pallas kernels for 11%

profile of v3, /device:TPU:32, one launch (start us, length us, event | category | flops | bytes accessed | tf_op | source)
XLA Modules:
  0.0 89.9 jit_solution(2999202971280467343)
XLA Ops:
  0.0 0.0 copy-start
  0.0 2.3 %shard_map.28 = (bf16[256,3584]{1,0:T(8,128)(2,1)S(1)}, bf16[256,1536]{1,0:T(8,128)(2,1)S(1)}, bf16[256,1536]{1,0:T(8,128)(2,1)S(1)}) custom-call(bf16[256,8192]{1,0:T(8,128)(2,1)} %a_own.3, bf16[256,512]{1,0:T(8,128)(2,1)} %g_own.3), custom_call_target="tpu_custom_call" | custom-call | tf_op jit(solution)/shard_map/pallas_call | solution.py:126
  2.3 1.9 %collective-permute-start = (bf16[256,3584]{1,0:T(8,128)(2,1)S(1)}, bf16[256,3584]{1,0:T(8,128)(2,1)S(1)}, u32[]{:S(2)}, u32[]{:S(2)}) collective-permute-start(bf16[256,3584]{1,0:T(8,128)(2,1)S(1)} %get-tuple-element.10), channel_id=1, source_target_pairs={{0,16},{16,0},{32,48},{48,32},{64,80},{80,64},{96,112},{112,96},{1... | collective-permute-start | bytes 5505032 | tf_op jit(solution)/shard_map/ppermute | solution.py:284
  4.2 4.9 %collective-permute-start.1 = (bf16[256,1536]{1,0:T(8,128)(2,1)S(1)}, bf16[256,1536]{1,0:T(8,128)(2,1)S(1)}, u32[]{:S(2)}, u32[]{:S(2)}) collective-permute-start(bf16[256,1536]{1,0:T(8,128)(2,1)S(1)} %get-tuple-element.11), channel_id=1, source_target_pairs={{0,64},{16,272},{32,96},{48,304},{64,0},{80,336},{96,32},{112,368}... | collective-permute-start | bytes 2359304 | tf_op jit(solution)/shard_map/ppermute | solution.py:285
  9.2 2.2 %collective-permute-start.2 = (bf16[256,1536]{1,0:T(8,128)(2,1)S(1)}, bf16[256,1536]{1,0:T(8,128)(2,1)S(1)}, u32[]{:S(2)}, u32[]{:S(2)}) collective-permute-start(bf16[256,1536]{1,0:T(8,128)(2,1)S(1)} %get-tuple-element.12), channel_id=1, source_target_pairs={{16,64},{0,272},{48,96},{32,304},{80,0},{64,336},{112,32},{96,368}... | collective-permute-start | bytes 2359304 | tf_op jit(solution)/shard_map/ppermute | solution.py:285
  11.4 0.0 collective-permute-done.swapped
  11.4 0.0 copy-done
  11.4 5.7 %shard_map.30 = (bf16[528,1024]{1,0:T(8,128)(2,1)S(1)}, bf16[528,1024]{1,0:T(8,128)(2,1)S(1)}) custom-call(bf16[256,512]{1,0:T(8,128)(2,1)S(1)} %copy-done, bf16[256,8192]{1,0:T(8,128)(2,1)} %a_own.3, bf16[256,3584]{1,0:T(8,128)(2,1)S(1)} %collective-permute-done.swapped), custom_call_target="tpu_custom_call" | custom-call | flops 2147483648 | bytes 1048576 | tf_op jit(solution)/shard_map/pallas_call | solution.py:174
  17.1 3.4 %collective-permute-start.3 = (bf16[528,1024]{1,0:T(8,128)(2,1)S(1)}, bf16[528,1024]{1,0:T(8,128)(2,1)S(1)}, u32[]{:S(2)}, u32[]{:S(2)}) collective-permute-start(bf16[528,1024]{1,0:T(8,128)(2,1)S(1)} %get-tuple-element.13), channel_id=1, source_target_pairs={{0,32},{16,144},{32,64},{48,176},{64,96},{80,208},{96,0},{112,240}... | collective-permute-start | bytes 3244040 | tf_op jit(solution)/shard_map/ppermute | solution.py:287
  20.5 3.6 %collective-permute-start.4 = (bf16[528,1024]{1,0:T(8,128)(2,1)S(1)}, bf16[528,1024]{1,0:T(8,128)(2,1)S(1)}, u32[]{:S(2)}, u32[]{:S(2)}) collective-permute-start(bf16[528,1024]{1,0:T(8,128)(2,1)S(1)} %get-tuple-element.14), channel_id=1, source_target_pairs={{0,96},{16,400},{32,0},{48,432},{64,32},{80,464},{96,64},{112,496}... | collective-permute-start | bytes 3244040 | tf_op jit(solution)/shard_map/ppermute | solution.py:288
  24.2 1.0 %collective-permute-done.1.rest_0_ = bf16[256,1536]{1,0:T(8,128)(2,1)S(1)} collective-permute-done((bf16[256,1536]{1,0:T(8,128)(2,1)S(1)}, bf16[256,1536]{1,0:T(8,128)(2,1)S(1)}, u32[]{:S(2)}, u32[]{:S(2)}) %collective-permute-start.1) | collective-permute-done | bytes 786464 | tf_op jit(solution)/shard_map/ppermute | solution.py:285
  25.2 6.0 %collective-permute-done.2.rest_1_ = bf16[256,1536]{1,0:T(8,128)(2,1)S(1)} collective-permute-done((bf16[256,1536]{1,0:T(8,128)(2,1)S(1)}, bf16[256,1536]{1,0:T(8,128)(2,1)S(1)}, u32[]{:S(2)}, u32[]{:S(2)}) %collective-permute-start.2) | collective-permute-done | bytes 786464 | tf_op jit(solution)/shard_map/ppermute | solution.py:285
  31.2 4.6 %shard_map.29.own = f32[512,1024]{1,0:T(8,128)S(1)} custom-call(bf16[256,512]{1,0:T(8,128)(2,1)S(1)} %copy-done, bf16[256,8192]{1,0:T(8,128)(2,1)} %a_own.3, bf16[256,3584]{1,0:T(8,128)(2,1)S(1)} %collective-permute-done.swapped, bf16[256,1536]{1,0:T(8,128)(2,1)S(1)} %collective-permute-done.1.rest_0_, bf16[256,1536]{1,0:T(8,128)(2,1)S(1)} %collective-permute-done.2.rest_1_), custom_call_target="tpu_custom_call" | custom-call | flops 68719476736 | bytes 1048576 | tf_op jit(solution)/shard_map/pallas_call | solution.py:174
  35.9 3.7 %collective-permute-done.3.r0 = bf16[528,1024]{1,0:T(8,128)(2,1)S(1)} collective-permute-done((bf16[528,1024]{1,0:T(8,128)(2,1)S(1)}, bf16[528,1024]{1,0:T(8,128)(2,1)S(1)}, u32[]{:S(2)}, u32[]{:S(2)}) %collective-permute-start.3) | collective-permute-done | bytes 1081376 | tf_op jit(solution)/shard_map/ppermute | solution.py:287
  39.6 0.1 collective-permute-done.4.r1
  39.7 1.0 %shard_map.31 = bf16[4,528,256]{2,1,0:T(8,128)(2,1)S(1)} custom-call(f32[512,1024]{1,0:T(8,128)S(1)} %shard_map.29.own, bf16[528,1024]{1,0:T(8,128)(2,1)S(1)} %collective-permute-done.3.r0, bf16[528,1024]{1,0:T(8,128)(2,1)S(1)} %collective-permute-done.4.r1), custom_call_target="tpu_custom_call" | custom-call | tf_op jit(solution)/shard_map/pallas_call | solution.py:209
  40.8 15.3 %all_to_all.10.got = bf16[4,528,256]{2,1,0:T(8,128)(2,1)S(1)} all-to-all(bf16[4,528,256]{2,1,0:T(8,128)(2,1)S(1)} %shard_map.31), channel_id=1, replica_groups={{0,128,256,384},{32,160,288,416},{64,192,320,448},{96,224,352,480},{16,..., dimensions={0} | all-to-all | bytes 2162688 | tf_op jit(solution)/shard_map/all_to_all | solution.py:291
  56.1 0.5 shard_map.32
  56.6 32.7 %all_to_all.11.got = bf16[16,64,128]{2,1,0:T(8,128)(2,1)S(1)} all-to-all(bf16[16,64,128]{2,1,0:T(8,128)(2,1)S(1)} %shard_map.32), channel_id=1, replica_groups=mesh['inner'=32,'outer'=16] {'outer'}, dimensions={0} | all-to-all | bytes 524288 | tf_op jit(solution)/shard_map/all_to_all | solution.py:295
  89.3 0.7 shard_map.33
Async XLA Ops:
  0.0 11.4 %copy-start = (bf16[256,512]{1,0:T(8,128)(2,1)S(1)}, bf16[256,512]{1,0:T(8,128)(2,1)}, u32[]{:S(2)}) copy-start(bf16[256,512]{1,0:T(8,128)(2,1)} %g_own.3) | copy-start | bytes 786436
  2.3 9.1 %collective-permute-start = (bf16[256,3584]{1,0:T(8,128)(2,1)S(1)}, bf16[256,3584]{1,0:T(8,128)(2,1)S(1)}, u32[]{:S(2)}, u32[]{:S(2)}) collective-permute-start(bf16[256,3584]{1,0:T(8,128)(2,1)S(1)} %get-tuple-element.10), channel_id=1, source_target_pairs={{0,16},{16,0},{32,48},{48,32},{64,80},{80,64},{96,112},{112,96},{1... | collective-permute-start | bytes 5505032 | tf_op jit(solution)/shard_map/ppermute | solution.py:284
  4.2 21.0 %collective-permute-start.1 = (bf16[256,1536]{1,0:T(8,128)(2,1)S(1)}, bf16[256,1536]{1,0:T(8,128)(2,1)S(1)}, u32[]{:S(2)}, u32[]{:S(2)}) collective-permute-start(bf16[256,1536]{1,0:T(8,128)(2,1)S(1)} %get-tuple-element.11), channel_id=1, source_target_pairs={{0,64},{16,272},{32,96},{48,304},{64,0},{80,336},{96,32},{112,368}... | collective-permute-start | bytes 2359304 | tf_op jit(solution)/shard_map/ppermute | solution.py:285
  9.2 22.1 %collective-permute-start.2 = (bf16[256,1536]{1,0:T(8,128)(2,1)S(1)}, bf16[256,1536]{1,0:T(8,128)(2,1)S(1)}, u32[]{:S(2)}, u32[]{:S(2)}) collective-permute-start(bf16[256,1536]{1,0:T(8,128)(2,1)S(1)} %get-tuple-element.12), channel_id=1, source_target_pairs={{16,64},{0,272},{48,96},{32,304},{80,0},{64,336},{112,32},{96,368}... | collective-permute-start | bytes 2359304 | tf_op jit(solution)/shard_map/ppermute | solution.py:285
  17.1 22.5 %collective-permute-start.3 = (bf16[528,1024]{1,0:T(8,128)(2,1)S(1)}, bf16[528,1024]{1,0:T(8,128)(2,1)S(1)}, u32[]{:S(2)}, u32[]{:S(2)}) collective-permute-start(bf16[528,1024]{1,0:T(8,128)(2,1)S(1)} %get-tuple-element.13), channel_id=1, source_target_pairs={{0,32},{16,144},{32,64},{48,176},{64,96},{80,208},{96,0},{112,240}... | collective-permute-start | bytes 3244040 | tf_op jit(solution)/shard_map/ppermute | solution.py:287
  20.5 19.2 %collective-permute-start.4 = (bf16[528,1024]{1,0:T(8,128)(2,1)S(1)}, bf16[528,1024]{1,0:T(8,128)(2,1)S(1)}, u32[]{:S(2)}, u32[]{:S(2)}) collective-permute-start(bf16[528,1024]{1,0:T(8,128)(2,1)S(1)} %get-tuple-element.14), channel_id=1, source_target_pairs={{0,96},{16,400},{32,0},{48,432},{64,32},{80,464},{96,64},{112,496}... | collective-permute-start | bytes 3244040 | tf_op jit(solution)/shard_map/ppermute | solution.py:288

commit v4 on v3

--- a/solution.py
+++ b/solution.py
@@ -281,10 +281,12 @@
     n_outer = lax.axis_size("outer")
     swap = [(i, i ^ 1) for i in range(2 * NX * NY)]
     to_swap, same, cross = to_send(activations, output_grads)
+    got_same = lax.ppermute(same, "inner", ring(2))
     swapped = lax.ppermute(to_swap, "inner", swap)
-    far = (lax.ppermute(same, "inner", ring(2)), lax.ppermute(cross, "inner", ring(2, cross=True)))
-    ahead, behind = sums((1, 3), output_grads, activations, swapped)
+    far = (got_same, lax.ppermute(cross, "inner", ring(2, cross=True)))
+    (ahead,) = sums((1,), output_grads, activations, swapped)
     got_ahead = lax.ppermute(ahead, "inner", ring(1))
+    (behind,) = sums((3,), output_grads, activations, swapped)
     got_behind = lax.ppermute(behind, "inner", ring(3))
     (own,) = sums((0,), output_grads, activations, swapped, far)
     coded = row_sum(own, got_ahead, got_behind)

time: 90.3 us -> 90.3 us (level)
  Pallas kernels: 14.8 us -> 15.8 us
  waiting for transfers between devices: 10.9 us -> 9.94 us
    ppermute x1, waiting for transfers between devices: 3.73 us -> 2.46 us  [shards(): got_ahead = lax.ppermute(ahead, 'inner', ring(1))]
    pallas_call x2 -> x3, Pallas kernels: 10.3 us -> 11.3 us  [sums(): pl.pallas_call(functools.partial(sums_kernel, ks, kept), in_specs=[WHOLE,...]
  transfers between devices with their start and end apart: 5 -> 5, of which waited for: 4 -> 4; matrix products, arithmetic and copies ran while one was open for 0% -> 0% of each run, Pallas kernels for 11% -> 13%
where the time goes in v4:
time: 90.3 us; the launch traced here: 89.9 us
  blocking collectives  48 us (53%)
  starting transfers between devices  16.1 us (18%)
  Pallas kernels  15.8 us (17%)
  waiting for transfers between devices  9.94 us (11%)
    all_to_all x1, blocking collectives, shards(): lax.all_to_all(packed, 'outer', split_axis=0, concat_axis=0, tiled=True)  32.7 us
    all_to_all x1, blocking collectives, shards(): lax.all_to_all(coded, 'inner', split_axis=0, concat_axis=0, tiled=True, a...  15.3 us
    pallas_call x3, Pallas kernels, sums(): pl.pallas_call(functools.partial(sums_kernel, ks, kept), in_specs=[WHOLE,...  11.3 us
    ppermute x1, waiting for transfers between devices, shards(): far = (got_same, lax.ppermute(cross, 'inner', ring(2, cross=True)))  7.3 us
    ppermute x1, starting transfers between devices, shards(): got_same = lax.ppermute(same, 'inner', ring(2))  4.93 us
    ppermute x1, starting transfers between devices, shards(): got_behind = lax.ppermute(behind, 'inner', ring(3))  3.65 us
    ppermute x1, starting transfers between devices, shards(): got_ahead = lax.ppermute(ahead, 'inner', ring(1))  3.4 us
    ppermute x1, waiting for transfers between devices, shards(): got_ahead = lax.ppermute(ahead, 'inner', ring(1))  2.46 us
  transfers between devices with their start and end apart: 5, of which 4 were waited for; matrix products, arithmetic and copies ran while one was open for 0% of the time, Pallas kernels for 13%

profile of v4, /device:TPU:32, one launch (start us, length us, event | category | flops | bytes accessed | tf_op | source)
XLA Modules:
  0.0 89.9 jit_solution(1447407668761042009)
XLA Ops:
  0.0 0.0 copy-start
  0.0 2.3 %shard_map.28 = (bf16[256,3584]{1,0:T(8,128)(2,1)S(1)}, bf16[256,1536]{1,0:T(8,128)(2,1)S(1)}, bf16[256,1536]{1,0:T(8,128)(2,1)S(1)}) custom-call(bf16[256,8192]{1,0:T(8,128)(2,1)} %a_own.5, bf16[256,512]{1,0:T(8,128)(2,1)} %g_own.5), custom_call_target="tpu_custom_call" | custom-call | tf_op jit(solution)/shard_map/pallas_call | solution.py:126
  2.3 1.9 %collective-permute-start = (bf16[256,3584]{1,0:T(8,128)(2,1)S(1)}, bf16[256,3584]{1,0:T(8,128)(2,1)S(1)}, u32[]{:S(2)}, u32[]{:S(2)}) collective-permute-start(bf16[256,3584]{1,0:T(8,128)(2,1)S(1)} %get-tuple-element.8), channel_id=1, source_target_pairs={{0,16},{16,0},{32,48},{48,32},{64,80},{80,64},{96,112},{112,96},{1... | collective-permute-start | bytes 5505032 | tf_op jit(solution)/shard_map/ppermute | solution.py:285
  4.2 4.9 %collective-permute-start.1 = (bf16[256,1536]{1,0:T(8,128)(2,1)S(1)}, bf16[256,1536]{1,0:T(8,128)(2,1)S(1)}, u32[]{:S(2)}, u32[]{:S(2)}) collective-permute-start(bf16[256,1536]{1,0:T(8,128)(2,1)S(1)} %get-tuple-element.9), channel_id=1, source_target_pairs={{0,64},{16,272},{32,96},{48,304},{64,0},{80,336},{96,32},{112,368}... | collective-permute-start | bytes 2359304 | tf_op jit(solution)/shard_map/ppermute | solution.py:284
  9.2 2.2 %collective-permute-start.2 = (bf16[256,1536]{1,0:T(8,128)(2,1)S(1)}, bf16[256,1536]{1,0:T(8,128)(2,1)S(1)}, u32[]{:S(2)}, u32[]{:S(2)}) collective-permute-start(bf16[256,1536]{1,0:T(8,128)(2,1)S(1)} %get-tuple-element.10), channel_id=1, source_target_pairs={{16,64},{0,272},{48,96},{32,304},{80,0},{64,336},{112,32},{96,368}... | collective-permute-start | bytes 2359304 | tf_op jit(solution)/shard_map/ppermute | solution.py:286
  11.4 0.0 collective-permute-done.swapped
  11.4 0.0 copy-done
  11.4 3.3 %shard_map.30 = bf16[528,1024]{1,0:T(8,128)(2,1)S(1)} custom-call(bf16[256,512]{1,0:T(8,128)(2,1)S(1)} %copy-done, bf16[256,8192]{1,0:T(8,128)(2,1)} %a_own.5, bf16[256,3584]{1,0:T(8,128)(2,1)S(1)} %collective-permute-done.swapped), custom_call_target="tpu_custom_call" | custom-call | flops 2147483648 | bytes 1048576 | tf_op jit(solution)/shard_map/pallas_call | solution.py:174
  14.7 3.4 %collective-permute-start.3 = (bf16[528,1024]{1,0:T(8,128)(2,1)S(1)}, bf16[528,1024]{1,0:T(8,128)(2,1)S(1)}, u32[]{:S(2)}, u32[]{:S(2)}) collective-permute-start(bf16[528,1024]{1,0:T(8,128)(2,1)S(1)} %shard_map.30), channel_id=1, source_target_pairs={{0,32},{16,144},{32,64},{48,176},{64,96},{80,208},{96,0},{112,240}... | collective-permute-start | bytes 3244040 | tf_op jit(solution)/shard_map/ppermute | solution.py:288
  18.1 3.3 %shard_map.31 = bf16[528,1024]{1,0:T(8,128)(2,1)S(1)} custom-call(bf16[256,512]{1,0:T(8,128)(2,1)S(1)} %copy-done, bf16[256,8192]{1,0:T(8,128)(2,1)} %a_own.5, bf16[256,3584]{1,0:T(8,128)(2,1)S(1)} %collective-permute-done.swapped), custom_call_target="tpu_custom_call" | custom-call | flops 2147483648 | bytes 1048576 | tf_op jit(solution)/shard_map/pallas_call | solution.py:174
  21.5 3.6 %collective-permute-start.4 = (bf16[528,1024]{1,0:T(8,128)(2,1)S(1)}, bf16[528,1024]{1,0:T(8,128)(2,1)S(1)}, u32[]{:S(2)}, u32[]{:S(2)}) collective-permute-start(bf16[528,1024]{1,0:T(8,128)(2,1)S(1)} %shard_map.31), channel_id=1, source_target_pairs={{0,96},{16,400},{32,0},{48,432},{64,32},{80,464},{96,64},{112,496}... | collective-permute-start | bytes 3244040 | tf_op jit(solution)/shard_map/ppermute | solution.py:290
  25.1 0.1 collective-permute-done.1.rest_0_
  25.2 7.3 %collective-permute-done.2.rest_1_ = bf16[256,1536]{1,0:T(8,128)(2,1)S(1)} collective-permute-done((bf16[256,1536]{1,0:T(8,128)(2,1)S(1)}, bf16[256,1536]{1,0:T(8,128)(2,1)S(1)}, u32[]{:S(2)}, u32[]{:S(2)}) %collective-permute-start.2) | collective-permute-done | bytes 786464 | tf_op jit(solution)/shard_map/ppermute | solution.py:286
  32.5 4.7 %shard_map.29.own = f32[512,1024]{1,0:T(8,128)S(1)} custom-call(bf16[256,512]{1,0:T(8,128)(2,1)S(1)} %copy-done, bf16[256,8192]{1,0:T(8,128)(2,1)} %a_own.5, bf16[256,3584]{1,0:T(8,128)(2,1)S(1)} %collective-permute-done.swapped, bf16[256,1536]{1,0:T(8,128)(2,1)S(1)} %collective-permute-done.1.rest_0_, bf16[256,1536]{1,0:T(8,128)(2,1)S(1)} %collective-permute-done.2.rest_1_), custom_call_target="tpu_custom_call" | custom-call | flops 68719476736 | bytes 1048576 | tf_op jit(solution)/shard_map/pallas_call | solution.py:174
  37.2 2.5 %collective-permute-done.3.r0 = bf16[528,1024]{1,0:T(8,128)(2,1)S(1)} collective-permute-done((bf16[528,1024]{1,0:T(8,128)(2,1)S(1)}, bf16[528,1024]{1,0:T(8,128)(2,1)S(1)}, u32[]{:S(2)}, u32[]{:S(2)}) %collective-permute-start.3) | collective-permute-done | bytes 1081376 | tf_op jit(solution)/shard_map/ppermute | solution.py:288
  39.6 0.1 collective-permute-done.4.r1
  39.7 1.0 %shard_map.32 = bf16[4,528,256]{2,1,0:T(8,128)(2,1)S(1)} custom-call(f32[512,1024]{1,0:T(8,128)S(1)} %shard_map.29.own, bf16[528,1024]{1,0:T(8,128)(2,1)S(1)} %collective-permute-done.3.r0, bf16[528,1024]{1,0:T(8,128)(2,1)S(1)} %collective-permute-done.4.r1), custom_call_target="tpu_custom_call" | custom-call | tf_op jit(solution)/shard_map/pallas_call | solution.py:209
  40.8 15.3 %all_to_all.10.got = bf16[4,528,256]{2,1,0:T(8,128)(2,1)S(1)} all-to-all(bf16[4,528,256]{2,1,0:T(8,128)(2,1)S(1)} %shard_map.32), channel_id=1, replica_groups={{0,128,256,384},{32,160,288,416},{64,192,320,448},{96,224,352,480},{16,..., dimensions={0} | all-to-all | bytes 2162688 | tf_op jit(solution)/shard_map/all_to_all | solution.py:293
  56.1 0.5 shard_map.33
  56.6 32.7 %all_to_all.11.got = bf16[16,64,128]{2,1,0:T(8,128)(2,1)S(1)} all-to-all(bf16[16,64,128]{2,1,0:T(8,128)(2,1)S(1)} %shard_map.33), channel_id=1, replica_groups=mesh['inner'=32,'outer'=16] {'outer'}, dimensions={0} | all-to-all | bytes 524288 | tf_op jit(solution)/shard_map/all_to_all | solution.py:297
  89.3 0.7 shard_map.34
Async XLA Ops:
  0.0 11.4 %copy-start = (bf16[256,512]{1,0:T(8,128)(2,1)S(1)}, bf16[256,512]{1,0:T(8,128)(2,1)}, u32[]{:S(2)}) copy-start(bf16[256,512]{1,0:T(8,128)(2,1)} %g_own.5) | copy-start | bytes 786436
  2.3 9.1 %collective-permute-start = (bf16[256,3584]{1,0:T(8,128)(2,1)S(1)}, bf16[256,3584]{1,0:T(8,128)(2,1)S(1)}, u32[]{:S(2)}, u32[]{:S(2)}) collective-permute-start(bf16[256,3584]{1,0:T(8,128)(2,1)S(1)} %get-tuple-element.8), channel_id=1, source_target_pairs={{0,16},{16,0},{32,48},{48,32},{64,80},{80,64},{96,112},{112,96},{1... | collective-permute-start | bytes 5505032 | tf_op jit(solution)/shard_map/ppermute | solution.py:285
  4.2 21.0 %collective-permute-start.1 = (bf16[256,1536]{1,0:T(8,128)(2,1)S(1)}, bf16[256,1536]{1,0:T(8,128)(2,1)S(1)}, u32[]{:S(2)}, u32[]{:S(2)}) collective-permute-start(bf16[256,1536]{1,0:T(8,128)(2,1)S(1)} %get-tuple-element.9), channel_id=1, source_target_pairs={{0,64},{16,272},{32,96},{48,304},{64,0},{80,336},{96,32},{112,368}... | collective-permute-start | bytes 2359304 | tf_op jit(solution)/shard_map/ppermute | solution.py:284
  9.2 23.3 %collective-permute-start.2 = (bf16[256,1536]{1,0:T(8,128)(2,1)S(1)}, bf16[256,1536]{1,0:T(8,128)(2,1)S(1)}, u32[]{:S(2)}, u32[]{:S(2)}) collective-permute-start(bf16[256,1536]{1,0:T(8,128)(2,1)S(1)} %get-tuple-element.10), channel_id=1, source_target_pairs={{16,64},{0,272},{48,96},{32,304},{80,0},{64,336},{112,32},{96,368}... | collective-permute-start | bytes 2359304 | tf_op jit(solution)/shard_map/ppermute | solution.py:286
  14.7 24.9 %collective-permute-start.3 = (bf16[528,1024]{1,0:T(8,128)(2,1)S(1)}, bf16[528,1024]{1,0:T(8,128)(2,1)S(1)}, u32[]{:S(2)}, u32[]{:S(2)}) collective-permute-start(bf16[528,1024]{1,0:T(8,128)(2,1)S(1)} %shard_map.30), channel_id=1, source_target_pairs={{0,32},{16,144},{32,64},{48,176},{64,96},{80,208},{96,0},{112,240}... | collective-permute-start | bytes 3244040 | tf_op jit(solution)/shard_map/ppermute | solution.py:288
  21.5 18.2 %collective-permute-start.4 = (bf16[528,1024]{1,0:T(8,128)(2,1)S(1)}, bf16[528,1024]{1,0:T(8,128)(2,1)S(1)}, u32[]{:S(2)}, u32[]{:S(2)}) collective-permute-start(bf16[528,1024]{1,0:T(8,128)(2,1)S(1)} %shard_map.31), channel_id=1, source_target_pairs={{0,96},{16,400},{32,0},{48,432},{64,32},{80,464},{96,64},{112,496}... | collective-permute-start | bytes 3244040 | tf_op jit(solution)/shard_map/ppermute | solution.py:290

commit v5 on v3

--- a/solution.py
+++ b/solution.py
@@ -65,14 +65,19 @@
     return total
 
 
-def put_coded(out, lanes, totals):
+def put_codes(out, start, totals):
     norms = []
     for b, total in enumerate(totals):
         code, norm = encode(total)
-        out[rows_of(b), lanes] = code
+        out[pl.ds(start + b * BLOCK, BLOCK), :] = code
         norms.append(norm.astype(F32))
+    return norms
+
+
+def put_coded(out, totals):
+    norms = put_codes(out, 0, totals)
     n = norms[0].shape[1]
-    out[COLS : COLS + TAIL, lanes] = jnp.concatenate(
+    out[COLS : COLS + TAIL, :] = jnp.concatenate(
         norms + [jnp.zeros((TAIL - NBLK, n), F32)], axis=0
     ).astype(BF16)
 
@@ -135,7 +140,7 @@
 
 def sums_kernel(ks, kept, g_own, a_own, swapped, *rest):
     n = len(ks)
-    far, outs, (abuf, gt, local, asem) = rest[: 2 * kept], rest[2 * kept : 2 * kept + n], rest[2 * kept + n :]
+    far, outs, (abuf, gt, local, nbuf, asem) = rest[: 2 * kept], rest[2 * kept : 2 * kept + n], rest[2 * kept + n :]
     devices = 2 + len(far)
 
     def a_in(m, q):
@@ -161,16 +166,21 @@
                 for b in range(NBLK):
                     outs[0][rows_of(b), lanes] = block_sum(local, b)
             else:
-                put_coded(outs[m], lanes, [block_sum(local, b) for b in range(NBLK)])
+                start = pl.multiple_of(q * COLS, COLS)
+                norms = put_codes(outs[m], start, [block_sum(local, b) for b in range(NBLK)])
+                nbuf[q] = jnp.concatenate(norms, axis=0)
             return carry
 
         lax.fori_loop(0, 4, step, 0)
+        if not kept:
+            packed = jnp.concatenate([nbuf[q] for q in range(4)], axis=0)
+            outs[m][4 * COLS :, :] = packed.astype(BF16)
 
 
 def sums(ks, g_own, a_own, swapped, far=()):
     n, tok, kept = len(ks), a_own.shape[0], len(far) > 0
     devices = 2 + len(far)
-    height, dtype = (COLS, F32) if kept else (COLS + TAIL, BF16)
+    shape, dtype = ((COLS, 4 * PART), F32) if kept else ((4 * COLS + TAIL, PART), BF16)
     return pl.pallas_call(
         functools.partial(sums_kernel, ks, kept),
         in_specs=[WHOLE, ANY, WHOLE] + [WHOLE] * len(far),
@@ -179,9 +189,10 @@
             pltpu.VMEM((4 * n, tok, PART), BF16),
             pltpu.VMEM((devices, COLS, tok), BF16),
             pltpu.VMEM((devices, COLS, PART), F32),
+            pltpu.VMEM((4, NBLK, PART), F32),
             pltpu.SemaphoreType.DMA((4 * n,)),
         ],
-        out_shape=[pltpu.VMEM((height, 4 * PART), dtype)] * n,
+        out_shape=[pltpu.VMEM(shape, dtype)] * n,
         compiler_params=PARAMS,
         cost_estimate=pl.CostEstimate(
             flops=2 ** (36 if kept else 31), bytes_accessed=2**20, transcendentals=0
@@ -189,17 +200,23 @@
     )(*near(g_own), pltpu.with_memory_space_constraint(a_own, HBM), *near(swapped, *far))
 
 
-def row_sum_kernel(own, r0, r1, out):
+def row_sum_kernel(own, r0, r1, out, nbuf):
+    for i, r in enumerate((r0, r1)):
+        norms = r[4 * COLS :, :].astype(F32)
+        for q in range(4):
+            nbuf[i, q] = norms[q * NBLK : (q + 1) * NBLK, :]
+
     def step(q, carry):
         lanes = lanes_of(q)
-        norms = [norms_of(r, lanes) for r in (r0, r1)]
+        start = pl.multiple_of(q * COLS, COLS)
         totals = []
         for b in range(NBLK):
             total = own[rows_of(b), lanes]
             for i, r in enumerate((r0, r1)):
-                total = total + get_coded(r, lanes, norms[i], b)
+                code = r[pl.ds(start + b * BLOCK, BLOCK), :]
+                total = total + decode(code, nbuf[i, q, b : b + 1, :])
             totals.append(total)
-        put_coded(out.at[q], slice(None), totals)
+        put_coded(out.at[q], totals)
         return carry
 
     lax.fori_loop(0, 4, step, 0)
@@ -211,6 +228,7 @@
         in_specs=[WHOLE] * 3,
         out_specs=WHOLE,
         out_shape=pltpu.VMEM((4, COLS + TAIL, PART), BF16),
+        scratch_shapes=[pltpu.VMEM((2, 4, NBLK, PART), F32)],
         compiler_params=PARAMS,
     )(*near(own, r0, r1))
 

time: 90.3 us -> 90 us (level)
  transfers between devices with their start and end apart: 5 -> 5, of which waited for: 4 -> 4; matrix products, arithmetic and copies ran while one was open for 0% -> 0% of each run, Pallas kernels for 11% -> 12%
where the time goes in v5:
time: 90 us; the launch traced here: 89.7 us
  blocking collectives  48 us (53%)
  starting transfers between devices  16.1 us (18%)
  Pallas kernels  14.8 us (16%)
  waiting for transfers between devices  10.6 us (12%)
    all_to_all x1, blocking collectives, shards(): lax.all_to_all(packed, 'outer', split_axis=0, concat_axis=0, tiled=True)  32.7 us
    all_to_all x1, blocking collectives, shards(): lax.all_to_all(coded, 'inner', split_axis=0, concat_axis=0, tiled=True, a...  15.3 us
    pallas_call x2, Pallas kernels, sums(): pl.pallas_call(functools.partial(sums_kernel, ks, kept), in_specs=[WHOLE,...  10.3 us
    ppermute x1, waiting for transfers between devices, shards(): lax.ppermute(cross, 'inner', ring(2, cross=True))  6.04 us
    ppermute x1, starting transfers between devices, shards(): lax.ppermute(same, 'inner', ring(2))  4.93 us
    ppermute x1, starting transfers between devices, shards(): got_behind = lax.ppermute(behind, 'inner', ring(3))  3.66 us
    ppermute x1, waiting for transfers between devices, shards(): got_ahead = lax.ppermute(ahead, 'inner', ring(1))  3.46 us
    ppermute x1, starting transfers between devices, shards(): got_ahead = lax.ppermute(ahead, 'inner', ring(1))  3.4 us
  transfers between devices with their start and end apart: 5, of which 4 were waited for; matrix products, arithmetic and copies ran while one was open for 0% of the time, Pallas kernels for 12%

profile of v5, /device:TPU:32, one launch (start us, length us, event | category | flops | bytes accessed | tf_op | source)
XLA Modules:
  0.0 89.7 jit_solution(14343418852716243711)
XLA Ops:
  0.0 0.0 copy-start
  0.0 2.3 %shard_map.28 = (bf16[256,3584]{1,0:T(8,128)(2,1)S(1)}, bf16[256,1536]{1,0:T(8,128)(2,1)S(1)}, bf16[256,1536]{1,0:T(8,128)(2,1)S(1)}) custom-call(bf16[256,8192]{1,0:T(8,128)(2,1)} %a_own.3, bf16[256,512]{1,0:T(8,128)(2,1)} %g_own.3), custom_call_target="tpu_custom_call" | custom-call | tf_op jit(solution)/shard_map/pallas_call | solution.py:131
  2.3 1.9 %collective-permute-start = (bf16[256,3584]{1,0:T(8,128)(2,1)S(1)}, bf16[256,3584]{1,0:T(8,128)(2,1)S(1)}, u32[]{:S(2)}, u32[]{:S(2)}) collective-permute-start(bf16[256,3584]{1,0:T(8,128)(2,1)S(1)} %get-tuple-element.10), channel_id=1, source_target_pairs={{0,16},{16,0},{32,48},{48,32},{64,80},{80,64},{96,112},{112,96},{1... | collective-permute-start | bytes 5505032 | tf_op jit(solution)/shard_map/ppermute | solution.py:302
  4.2 4.9 %collective-permute-start.1 = (bf16[256,1536]{1,0:T(8,128)(2,1)S(1)}, bf16[256,1536]{1,0:T(8,128)(2,1)S(1)}, u32[]{:S(2)}, u32[]{:S(2)}) collective-permute-start(bf16[256,1536]{1,0:T(8,128)(2,1)S(1)} %get-tuple-element.11), channel_id=1, source_target_pairs={{0,64},{16,272},{32,96},{48,304},{64,0},{80,336},{96,32},{112,368}... | collective-permute-start | bytes 2359304 | tf_op jit(solution)/shard_map/ppermute | solution.py:303
  9.2 2.2 %collective-permute-start.2 = (bf16[256,1536]{1,0:T(8,128)(2,1)S(1)}, bf16[256,1536]{1,0:T(8,128)(2,1)S(1)}, u32[]{:S(2)}, u32[]{:S(2)}) collective-permute-start(bf16[256,1536]{1,0:T(8,128)(2,1)S(1)} %get-tuple-element.12), channel_id=1, source_target_pairs={{16,64},{0,272},{48,96},{32,304},{80,0},{64,336},{112,32},{96,368}... | collective-permute-start | bytes 2359304 | tf_op jit(solution)/shard_map/ppermute | solution.py:303
  11.4 0.0 collective-permute-done.swapped
  11.4 0.0 copy-done
  11.4 5.7 %shard_map.30 = (bf16[2064,256]{1,0:T(8,128)(2,1)S(1)}, bf16[2064,256]{1,0:T(8,128)(2,1)S(1)}) custom-call(bf16[256,512]{1,0:T(8,128)(2,1)S(1)} %copy-done, bf16[256,8192]{1,0:T(8,128)(2,1)} %a_own.3, bf16[256,3584]{1,0:T(8,128)(2,1)S(1)} %collective-permute-done.swapped), custom_call_target="tpu_custom_call" | custom-call | flops 2147483648 | bytes 1048576 | tf_op jit(solution)/shard_map/pallas_call | solution.py:184
  17.1 3.4 %collective-permute-start.3 = (bf16[2064,256]{1,0:T(8,128)(2,1)S(1)}, bf16[2064,256]{1,0:T(8,128)(2,1)S(1)}, u32[]{:S(2)}, u32[]{:S(2)}) collective-permute-start(bf16[2064,256]{1,0:T(8,128)(2,1)S(1)} %get-tuple-element.13), channel_id=1, source_target_pairs={{0,32},{16,144},{32,64},{48,176},{64,96},{80,208},{96,0},{112,240}... | collective-permute-start | bytes 3170312 | tf_op jit(solution)/shard_map/ppermute | solution.py:305
  20.5 3.7 %collective-permute-start.4 = (bf16[2064,256]{1,0:T(8,128)(2,1)S(1)}, bf16[2064,256]{1,0:T(8,128)(2,1)S(1)}, u32[]{:S(2)}, u32[]{:S(2)}) collective-permute-start(bf16[2064,256]{1,0:T(8,128)(2,1)S(1)} %get-tuple-element.14), channel_id=1, source_target_pairs={{0,96},{16,400},{32,0},{48,432},{64,32},{80,464},{96,64},{112,496}... | collective-permute-start | bytes 3170312 | tf_op jit(solution)/shard_map/ppermute | solution.py:306
  24.2 1.0 %collective-permute-done.1.rest_0_ = bf16[256,1536]{1,0:T(8,128)(2,1)S(1)} collective-permute-done((bf16[256,1536]{1,0:T(8,128)(2,1)S(1)}, bf16[256,1536]{1,0:T(8,128)(2,1)S(1)}, u32[]{:S(2)}, u32[]{:S(2)}) %collective-permute-start.1) | collective-permute-done | bytes 786464 | tf_op jit(solution)/shard_map/ppermute | solution.py:303
  25.2 6.0 %collective-permute-done.2.rest_1_ = bf16[256,1536]{1,0:T(8,128)(2,1)S(1)} collective-permute-done((bf16[256,1536]{1,0:T(8,128)(2,1)S(1)}, bf16[256,1536]{1,0:T(8,128)(2,1)S(1)}, u32[]{:S(2)}, u32[]{:S(2)}) %collective-permute-start.2) | collective-permute-done | bytes 786464 | tf_op jit(solution)/shard_map/ppermute | solution.py:303
  31.2 4.6 %shard_map.29.own = f32[512,1024]{1,0:T(8,128)S(1)} custom-call(bf16[256,512]{1,0:T(8,128)(2,1)S(1)} %copy-done, bf16[256,8192]{1,0:T(8,128)(2,1)} %a_own.3, bf16[256,3584]{1,0:T(8,128)(2,1)S(1)} %collective-permute-done.swapped, bf16[256,1536]{1,0:T(8,128)(2,1)S(1)} %collective-permute-done.1.rest_0_, bf16[256,1536]{1,0:T(8,128)(2,1)S(1)} %collective-permute-done.2.rest_1_), custom_call_target="tpu_custom_call" | custom-call | flops 68719476736 | bytes 1048576 | tf_op jit(solution)/shard_map/pallas_call | solution.py:184
  35.9 3.5 %collective-permute-done.3.r0 = bf16[2064,256]{1,0:T(8,128)(2,1)S(1)} collective-permute-done((bf16[2064,256]{1,0:T(8,128)(2,1)S(1)}, bf16[2064,256]{1,0:T(8,128)(2,1)S(1)}, u32[]{:S(2)}, u32[]{:S(2)}) %collective-permute-start.3) | collective-permute-done | bytes 1056800 | tf_op jit(solution)/shard_map/ppermute | solution.py:305
  39.4 0.1 collective-permute-done.4.r1
  39.4 1.0 %shard_map.31 = bf16[4,528,256]{2,1,0:T(8,128)(2,1)S(1)} custom-call(f32[512,1024]{1,0:T(8,128)S(1)} %shard_map.29.own, bf16[2064,256]{1,0:T(8,128)(2,1)S(1)} %collective-permute-done.3.r0, bf16[2064,256]{1,0:T(8,128)(2,1)S(1)} %collective-permute-done.4.r1), custom_call_target="tpu_custom_call" | custom-call | tf_op jit(solution)/shard_map/pallas_call | solution.py:226
  40.5 15.3 %all_to_all.10.got = bf16[4,528,256]{2,1,0:T(8,128)(2,1)S(1)} all-to-all(bf16[4,528,256]{2,1,0:T(8,128)(2,1)S(1)} %shard_map.31), channel_id=1, replica_groups={{0,128,256,384},{32,160,288,416},{64,192,320,448},{96,224,352,480},{16,..., dimensions={0} | all-to-all | bytes 2162688 | tf_op jit(solution)/shard_map/all_to_all | solution.py:309
  55.8 0.5 shard_map.32
  56.3 32.7 %all_to_all.11.got = bf16[16,64,128]{2,1,0:T(8,128)(2,1)S(1)} all-to-all(bf16[16,64,128]{2,1,0:T(8,128)(2,1)S(1)} %shard_map.32), channel_id=1, replica_groups=mesh['inner'=32,'outer'=16] {'outer'}, dimensions={0} | all-to-all | bytes 524288 | tf_op jit(solution)/shard_map/all_to_all | solution.py:313
  89.0 0.7 shard_map.33
Async XLA Ops:
  0.0 11.4 %copy-start = (bf16[256,512]{1,0:T(8,128)(2,1)S(1)}, bf16[256,512]{1,0:T(8,128)(2,1)}, u32[]{:S(2)}) copy-start(bf16[256,512]{1,0:T(8,128)(2,1)} %g_own.3) | copy-start | bytes 786436
  2.3 9.1 %collective-permute-start = (bf16[256,3584]{1,0:T(8,128)(2,1)S(1)}, bf16[256,3584]{1,0:T(8,128)(2,1)S(1)}, u32[]{:S(2)}, u32[]{:S(2)}) collective-permute-start(bf16[256,3584]{1,0:T(8,128)(2,1)S(1)} %get-tuple-element.10), channel_id=1, source_target_pairs={{0,16},{16,0},{32,48},{48,32},{64,80},{80,64},{96,112},{112,96},{1... | collective-permute-start | bytes 5505032 | tf_op jit(solution)/shard_map/ppermute | solution.py:302
  4.2 21.0 %collective-permute-start.1 = (bf16[256,1536]{1,0:T(8,128)(2,1)S(1)}, bf16[256,1536]{1,0:T(8,128)(2,1)S(1)}, u32[]{:S(2)}, u32[]{:S(2)}) collective-permute-start(bf16[256,1536]{1,0:T(8,128)(2,1)S(1)} %get-tuple-element.11), channel_id=1, source_target_pairs={{0,64},{16,272},{32,96},{48,304},{64,0},{80,336},{96,32},{112,368}... | collective-permute-start | bytes 2359304 | tf_op jit(solution)/shard_map/ppermute | solution.py:303
  9.2 22.1 %collective-permute-start.2 = (bf16[256,1536]{1,0:T(8,128)(2,1)S(1)}, bf16[256,1536]{1,0:T(8,128)(2,1)S(1)}, u32[]{:S(2)}, u32[]{:S(2)}) collective-permute-start(bf16[256,1536]{1,0:T(8,128)(2,1)S(1)} %get-tuple-element.12), channel_id=1, source_target_pairs={{16,64},{0,272},{48,96},{32,304},{80,0},{64,336},{112,32},{96,368}... | collective-permute-start | bytes 2359304 | tf_op jit(solution)/shard_map/ppermute | solution.py:303
  17.1 22.2 %collective-permute-start.3 = (bf16[2064,256]{1,0:T(8,128)(2,1)S(1)}, bf16[2064,256]{1,0:T(8,128)(2,1)S(1)}, u32[]{:S(2)}, u32[]{:S(2)}) collective-permute-start(bf16[2064,256]{1,0:T(8,128)(2,1)S(1)} %get-tuple-element.13), channel_id=1, source_target_pairs={{0,32},{16,144},{32,64},{48,176},{64,96},{80,208},{96,0},{112,240}... | collective-permute-start | bytes 3170312 | tf_op jit(solution)/shard_map/ppermute | solution.py:305
  20.5 18.9 %collective-permute-start.4 = (bf16[2064,256]{1,0:T(8,128)(2,1)S(1)}, bf16[2064,256]{1,0:T(8,128)(2,1)S(1)}, u32[]{:S(2)}, u32[]{:S(2)}) collective-permute-start(bf16[2064,256]{1,0:T(8,128)(2,1)S(1)} %get-tuple-element.14), channel_id=1, source_target_pairs={{0,96},{16,400},{32,0},{48,432},{64,32},{80,464},{96,64},{112,496}... | collective-permute-start | bytes 3170312 | tf_op jit(solution)/shard_map/ppermute | solution.py:306
